TPU v7x, 128 devices: a whole 4x4x4 slice. The times are simulated.
128 devices in a mesh: dp: 2 (over core), ctx: 8 (over z, x_lo), tp: 8 (over x_hi, y).
Axes of the slice: x: 4 (x_hi: 2, x_lo: 2; x = x_hi * 2 + x_lo), y: 4, z: 4, core: 2. Of those that a mesh axis runs over, the one named last changes fastest.
Arguments:
- clean: bfloat16 [2, 2048, 5120], P('dp', 'ctx'), may hold values from -6 to 6
- noise: bfloat16 [2, 2048, 5120], P('dp', 'ctx'), may hold values from -6 to 6
- timestep: int32 [2], P('dp'), may hold values from 200 to 999
- teacher_gain: float32 [5120], replicated, may hold values from 0.7 to 2.8
- critic_gain: float32 [5120], replicated, may hold values from 0.7 to 2.8
- teacher_qkv: bfloat16 [5120, 3, 3072], P('dp', None, 'tp'), may hold values from -0.11879111 to 0.11879111
- critic_qkv: bfloat16 [5120, 3, 3072], P('dp', None, 'tp'), may hold values from -0.11879111 to 0.11879111
- teacher_out: bfloat16 [3072, 5120], P('tp', 'dp'), may hold values from -0.625 to 0.625
- critic_out: bfloat16 [3072, 5120], P('tp', 'dp'), may hold values from -0.625 to 0.625
Outputs:
- kl_grad: bfloat16 [2, 2048, 5120], P('dp', 'ctx', 'tp')
All inputs are finite; a program needn't handle non-finite values.
Results may differ from a plain program's by a relative error of at most 0.019.
The roundings to bfloat16 on the way count: a program that leaves them out, or rounds other values in their place, can miss the bound.
Values may be sent and summed in bfloat16 or wider, within the bound.
No kernel may reach another device: no remote copies, remote signals or barrier semaphores. Data moves between devices by JAX's collectives and lax.ppermute only.
A program may use at most 128 MiB of HBM per device.

v0:
```python
import jax
import jax.numpy as jnp
import numpy as np
from jax import lax
from jax.experimental import pallas as pl
from jax.experimental.pallas import tpu as pltpu
from jax.sharding import PartitionSpec as P

HD = 128
MIB = 1024 * 1024


def swapped(value):
    return lax.ppermute(value, "dp", [(0, 1), (1, 0)])


def exchange(value, axes):
    return lax.all_to_all(value, axes, 0, 0, tiled=True)


def in_hbm(value):
    return pltpu.with_memory_space_constraint(value, pltpu.HBM)


def in_vmem(value):
    return pltpu.with_memory_space_constraint(value, pltpu.VMEM)


SCALAR = pl.BlockSpec(memory_space=pltpu.SMEM)
NEAR = pl.BlockSpec(memory_space=pltpu.VMEM)
ANYWHERE = pl.BlockSpec(memory_space=pl.ANY)


def kernel(body, name, info, far, near, made, mib, flops, size, exps=0, scratch=(), loose=(), aliases=None):
    return pl.pallas_call(
        body,
        in_specs=[SCALAR] + [ANYWHERE] * len(far) + [NEAR] * len(near),
        out_specs=[NEAR] * len(made) + [ANYWHERE] * len(loose),
        out_shape=[pltpu.VMEM(shape, dtype) for shape, dtype in made]
        + [pltpu.HBM(shape, dtype) for shape, dtype in loose],
        scratch_shapes=list(scratch),
        input_output_aliases=aliases or {},
        compiler_params=pltpu.CompilerParams(vmem_limit_bytes=mib * MIB),
        cost_estimate=pl.CostEstimate(flops=flops, bytes_accessed=size, transcendentals=exps),
        name=name,
    )(
        info,
        *far,
        *[in_vmem(x) for x in near],
    )


BF16, F32 = jnp.bfloat16, jnp.float32

AT_CORE, AT_CTX, AT_STEP = range(3)


def noise_level(info_ref):
    step = (jnp.full((1, 1), info_ref[AT_STEP], jnp.int32).astype(F32) + 1.0) / 1000.0
    return 5.0 * step / (1.0 + 4.0 * step)


def norm_kernel(
    info_ref, clean_ref, noise_ref, gt_ref, gc_ref, w_ref,
    keep_ref, send_ref, held_ref,
    clean_buf, noise_buf, noisy_ref, gt_buf, gc_buf, in_sem, w_sem,
):
    tokens, width = clean_buf.shape
    rows = noisy_ref.shape[0]
    count = tokens // rows
    half = width // 2
    core = info_ref[AT_CORE]

    def arrival(i):
        part = pl.ds(pl.multiple_of(i * rows, rows), rows)
        return (
            pltpu.make_async_copy(clean_ref.at[part], clean_buf.at[part], in_sem.at[0, i]),
            pltpu.make_async_copy(noise_ref.at[part], noise_buf.at[part], in_sem.at[1, i]),
        )

    kinds = w_ref.shape[0]
    held = [
        pltpu.make_async_copy(w_ref.at[j], held_ref.at[j], w_sem.at[j]) for j in range(kinds)
    ]
    gains = [
        pltpu.make_async_copy(gt_ref, gt_buf, w_sem.at[kinds]),
        pltpu.make_async_copy(gc_ref, gc_buf, w_sem.at[kinds + 1]),
    ]
    for copy in gains:
        copy.start()
    for i in range(count):
        for copy in arrival(i):
            copy.start()
    for copy in held:
        copy.start()
    level = noise_level(info_ref)
    for copy in gains:
        copy.wait()

    @pl.loop(0, count)
    def _(i):
        for copy in arrival(i):
            copy.wait()
        part = pl.ds(pl.multiple_of(i * rows, rows), rows)
        squares = jnp.zeros((rows, HD), F32)
        for t in range(width // HD):
            columns = slice(t * HD, (t + 1) * HD)
            noisy = (1.0 - level) * clean_buf[part, columns].astype(
                F32
            ) + level * noise_buf[part, columns].astype(F32)
            noisy_ref[:, columns] = noisy
            squares += noisy * noisy
        mean = jnp.sum(squares, axis=-1, keepdims=True) / width
        inverse = jnp.broadcast_to(lax.rsqrt(mean + 1e-06), (rows, HD))
        place = lax.rem(i + core * (count // 2), count)
        place = pl.ds(pl.multiple_of(place * rows, rows), rows)
        for out, which in ((send_ref, 1 - core), (keep_ref, core)):
            for t in range(half // HD):
                tile = which * (half // HD) + t
                columns = pl.ds(pl.multiple_of(tile * HD, HD), HD)
                scaled = noisy_ref[:, columns] * inverse
                out[0, place, t * HD : (t + 1) * HD] = (
                    scaled * gt_buf[pl.ds(tile, 1), :]
                ).astype(BF16)
                out[1, place, t * HD : (t + 1) * HD] = (
                    scaled * gc_buf[pl.ds(tile, 1), :]
                ).astype(BF16)

    for copy in held:
        copy.wait()


def norm(info, clean, noise, gt, gc, w):
    tokens, width = clean.shape
    rows = 32
    count = tokens // rows
    tiles = (width // HD, HD)
    shape = ((2, tokens, width // 2), BF16)
    return kernel(
        norm_kernel,
        "norm",
        info,
        tuple(in_hbm(x) for x in (clean, noise, gt.reshape(tiles), gc.reshape(tiles), w)),
        (),
        (shape, shape, (w.shape, w.dtype)),
        16,
        10 * tokens * width,
        8 * tokens * width,
        scratch=(
            pltpu.VMEM((tokens, width), BF16),
            pltpu.VMEM((tokens, width), BF16),
            pltpu.VMEM((rows, width), F32),
            pltpu.VMEM(tiles, F32),
            pltpu.VMEM(tiles, F32),
            pltpu.SemaphoreType.DMA((2, count)),
            pltpu.SemaphoreType.DMA((w.shape[0] + 2,)),
        ),
    )


def project(info, model, a, weights, hold=None, fetch=None):
    _, tokens, depth = a.shape
    panel = weights[0].shape[-1]
    kinds = 3
    shape = ((kinds, tokens // 2, panel), F32)
    made = (shape, shape)
    if hold is not None:
        made += (((kinds - 1, depth, panel), BF16),)
    if fetch is not None:
        made += (((1, depth, panel), BF16),)
    far = tuple(in_hbm(w) for w in (hold, fetch) if w is not None)

    def body(info_ref, *refs):
        sources, rest = refs[: len(far)], refs[len(far) :]
        a_ref, *w_refs = rest[: 1 + len(weights)]
        top_ref, bottom_ref, *brought, sem = rest[1 + len(weights) :]
        first = 0 if fetch is None else kinds - 1
        copies = [
            pltpu.make_async_copy(sources[0].at[first + j], brought[0].at[j], sem.at[j])
            for j in range(brought[0].shape[0] if far else 0)
        ]
        for copy in copies:
            copy.start()

        def product(slices, j):
            value = jnp.dot(
                a_ref[model], jnp.concatenate(slices, axis=1), preferred_element_type=F32
            )
            for n in range(len(slices)):
                part = value[:, n * panel : (n + 1) * panel]
                top_ref[j + n] = part[: tokens // 2]
                bottom_ref[j + n] = part[tokens // 2 :]

        product([w[j] for w in w_refs for j in range(w.shape[0])], 0)
        for copy in copies:
            copy.wait()
        if fetch is not None:
            product([brought[0][0]], kinds - 1)

    return kernel(
        body,
        "project",
        info,
        far,
        (a, *weights),
        made,
        8,
        2 * tokens * depth * panel * kinds,
        2 * depth * (tokens + panel * kinds),
        scratch=(pltpu.SemaphoreType.DMA((kinds,)),),
    )


UNITS = 8


def join(info, model, parts, blocks=None):
    _, rows, panel = parts[0].shape
    half = rows // 2
    shape = (UNITS, 5 * rows + half, HD)

    def body(info_ref, *refs):
        target, out, sem = refs[-3:]
        inputs = refs[-3 - len(parts) : -3]
        copies = []
        for which in range(2):
            left, right = inputs[2 * which : 2 * which + 2]
            clip = info_ref[AT_CORE] if which == 0 else 1 - info_ref[AT_CORE]
            for kind, base in ((1, 0), (2, 2 * rows), (0, 4 * rows)):
                value = (left[kind] + right[kind]).astype(BF16)
                for j in range(2):
                    block = 2 * which + j
                    out[block, base : base + rows] = value[:, 2 * j * HD : (2 * j + 1) * HD]
                    middle = value[:, HD : 2 * HD]
                    if kind == 0:
                        middle = middle[j * half : (j + 1) * half]
                    out[block, base + rows : base + rows + middle.shape[0]] = middle
            copies.append(
                pltpu.make_async_copy(
                    out.at[pl.ds(2 * which, 2)],
                    target.at[pl.ds(4 * model + 2 * clip, 2)],
                    sem.at[which],
                )
            )
            copies[-1].start()
        for copy in copies:
            copy.wait()

    return kernel(
        body,
        "join",
        info,
        () if blocks is None else (blocks,),
        parts,
        (),
        8,
        6 * rows * panel,
        60 * rows * panel,
        scratch=(pltpu.VMEM((4, *shape[1:]), BF16), pltpu.SemaphoreType.DMA((2,))),
        loose=((shape, BF16),),
        aliases={} if blocks is None else {1: 0},
    )[0]


FACTOR = float(np.log2(np.e)) * HD**-0.5


def attend(info, queries, pairs, hold, state=None):
    _, size, _ = queries.shape
    half = size // 11
    rows = 2 * half
    tokens, length = 3 * half * UNITS, rows * UNITS
    step = 256
    count = len(hold)
    tasks = [
        (middle, held, g)
        for middle, held in ((0, rows), (1, half))
        for g in range(0, UNITS, step // held)
    ]

    def body(info_ref, *refs):
        sources, (q_ref, kv_ref, *rest) = refs[:count], refs[count:]
        before = ()
        if state is not None:
            before, rest = rest[:3], rest[3:]
        held_refs, rest = rest[:count], rest[count:]
        *outs, sem = rest
        holding = [
            pltpu.make_async_copy(source, place, sem.at[i])
            for i, (source, place) in enumerate(zip(sources, held_refs))
        ]
        for copy in holding:
            copy.start()
        sign = 1.0 - 2.0 * (info_ref[AT_CTX] // 4).astype(F32)

        def tokens_of(kind, middle):
            first = (kind + middle) * rows
            return kv_ref[:, first : first + rows].reshape(length, HD)

        def score(middle, held, g):
            first = (4 + middle) * rows
            query = q_ref[g : g + step // held, first : first + held].reshape(step, HD)
            return lax.dot_general(
                query, tokens_of(0, middle), (((1,), (1,)), ((), ())), preferred_element_type=F32
            )

        coming = score(*tasks[0])
        for n, (middle, held, g) in enumerate(tasks):
            current = coming
            if n + 1 < len(tasks):
                coming = score(*tasks[n + 1])
            lines = slice(n * step, (n + 1) * step)
            peak = jnp.broadcast_to(jnp.max(current, axis=-1, keepdims=True), (step, HD))
            if state is not None:
                old = before[0][lines, :]
                peak = jnp.maximum(peak, old)
            wide = jnp.concatenate([peak] * (length // HD), axis=1)
            weights = jnp.exp2((current - wide) * FACTOR)
            total = jnp.broadcast_to(jnp.sum(weights, axis=-1, keepdims=True), (step, HD))
            summed = jnp.dot(
                weights.astype(BF16), tokens_of(2, middle), preferred_element_type=F32
            )
            if state is None:
                outs[0][lines, :] = peak
                outs[1][lines, :] = total
                outs[2][lines, :] = summed
                continue
            scale = jnp.exp2((old - peak) * FACTOR)
            total = total + before[1][lines, :] * scale
            summed = summed + before[2][lines, :] * scale
            several = step // held
            outs[0][g : g + several, middle * rows : middle * rows + held] = (
                (summed * (sign / total)).astype(BF16).reshape(several, held, HD)
            )
        if state is not None:
            outs[1][...] = jnp.broadcast_to(noise_level(info_ref), (8, HD))
        for copy in holding:
            copy.wait()

    shape = ((UNITS, 3 * half, HD), BF16)
    made = tuple((h.shape, BF16) for h in hold)
    return kernel(
        body,
        "attend",
        info,
        tuple(hold),
        (queries, pairs, *(state or ())),
        made + ((((tokens, HD), F32),) * 3 if state is None else (shape, ((8, HD), F32))),
        24,
        4 * tokens * length * HD,
        4 * HD * (tokens + length),
        tokens * length,
        scratch=(pltpu.SemaphoreType.DMA((count,)),),
    )


def expand(info, attn, mine, other):
    _, size, _ = attn.shape
    half = size // 3
    rows, panel = 2 * half, 3 * HD
    columns = mine[0].shape[1]
    part = columns // 4
    shape = ((2 * UNITS, rows, part), BF16)

    def body(info_ref, attn_ref, *refs):
        weights, (out, left) = refs[:4], refs[4:]
        for unit in range(UNITS):
            model, clip, j = unit // 4, unit // 2 % 2, unit % 2
            line, lane = clip * rows, model * panel
            left[line : line + rows, lane + 2 * j * HD : lane + (2 * j + 1) * HD] = attn_ref[
                unit, :rows
            ]
            line += j * half
            left[line : line + half, lane + HD : lane + 2 * HD] = attn_ref[unit, rows:]
        for i in range(0, 8, 2):
            place = slice(i % 4 * part, (i % 4 + 2) * part)
            right = jnp.concatenate([w[:, place] for w in weights[i // 4 * 2 : i // 4 * 2 + 2]])
            value = jnp.dot(left[...], right, preferred_element_type=F32).astype(BF16)
            way = info_ref[AT_CORE] if i < 4 else 1 - info_ref[AT_CORE]
            for clip in range(2):
                block = clip * UNITS + way * 4 + i % 4
                for n in range(2):
                    out[block + n] = value[
                        clip * rows : (clip + 1) * rows, n * part : (n + 1) * part
                    ]

    return kernel(
        body,
        "expand",
        info,
        (),
        (attn, *mine, *other),
        (shape,),
        12,
        16 * rows * panel * columns,
        8 * panel * columns,
        scratch=(pltpu.VMEM((2 * rows, 2 * panel), BF16),),
    )[0]


def collect(level, blocks):
    _, rows, width = blocks.shape

    def body(level_ref, block_ref, out_ref):
        level = level_ref[:1, :1]
        step = 32
        for core in range(2):
            for line in range(0, rows, step):
                place = slice(line, line + step)
                total = block_ref[core * UNITS, place].astype(F32)
                for tp in range(1, UNITS):
                    total = total + block_ref[core * UNITS + tp, place].astype(F32)
                out_ref[core * rows + line : core * rows + line + step] = (level * total).astype(
                    BF16
                )

    return pl.pallas_call(
        body,
        in_specs=[NEAR, NEAR],
        out_specs=NEAR,
        out_shape=jax.ShapeDtypeStruct((2 * rows, width), BF16),
        compiler_params=pltpu.CompilerParams(vmem_limit_bytes=8 * MIB),
        name="collect",
    )(in_vmem(level), in_vmem(blocks))


def local(
    clean,
    noise,
    timestep,
    teacher_gain,
    critic_gain,
    teacher_qkv,
    critic_qkv,
    teacher_out,
    critic_out,
):
    places = [lax.axis_index("dp"), lax.axis_index("ctx"), timestep[0]]
    info = lax.optimization_barrier(jnp.stack(places).astype(jnp.int32))

    weights = [jnp.transpose(w, (1, 0, 2)) for w in (teacher_qkv, critic_qkv)]
    keep, away, weights_t = norm(
        info, clean[0], noise[0], teacher_gain, critic_gain, weights[0]
    )
    came = swapped(away)
    *own_t, most_c = project(info, 0, keep, (weights_t,), hold=weights[1])
    outs = (teacher_out, critic_out)
    other = [swapped(out) for out in outs]
    *own_c, last_c = project(info, 1, keep, (most_c,), fetch=weights[1])
    cross_t = project(info, 0, came, (weights_t,))
    cross_c = project(info, 1, came, (most_c, last_c))
    blocks = None
    for m, (own, cross) in enumerate(((own_t, cross_t), (own_c, cross_c))):
        parts = (own[0], swapped(cross[0]), cross[1], swapped(own[1]))
        blocks = join(info, m, parts, blocks)

    block = exchange(blocks, "ctx")
    *mine, peak, total, summed = attend(info, block, block, [in_hbm(out) for out in outs])
    *other, attn, level = attend(info, block, swapped(block), other, (peak, total, summed))
    sums = expand(info, exchange(attn, "ctx"), mine, other)
    return collect(level, exchange(sums, ("dp", "tp")))[None]


def solution(mesh):
    placed = (
        P("dp", "ctx", None),
        P("dp", "ctx", None),
        P("dp"),
        P(),
        P(),
        P("dp", None, "tp"),
        P("dp", None, "tp"),
        P("tp", "dp"),
        P("tp", "dp"),
    )
    return jax.shard_map(
        local, mesh=mesh, in_specs=placed, out_specs=P("dp", "ctx", "tp"), check_vma=False
    )
```

profile of v0, /device:TPU:1, one launch (start us, length us, event | category | flops | bytes accessed | tf_op | source)
XLA Modules:
  0.0 112.8 jit_solution(13813313887339057746)
XLA Ops:
  0.7 0.1 pad_add_fusion.info_ref
  0.7 5.1 %norm.1 = (bf16[2,256,2560]{2,1,0:T(8,128)(2,1)S(1)}, bf16[2,256,2560]{2,1,0:T(8,128)(2,1)S(1)}, bf16[3,2560,384]{2,1,0:T(8,128)(2,1)S(1)}) custom-call(s32[3]{0:T(128)S(1)} %pad_add_fusion.info_ref, bf16[256,5120]{1,0:T(8,128)(2,1)} %bitcast.12, bf16[256,5120]{1,0:T(8,128)(2,1)} %bitcast.13, f32[40,128]{1,0:T(8,128)} %bitcast.14, f32[40,128]{1,0:T(8,128)} %bitcast.15, ...), custom_call_target="tpu_custom_call" | custom-call | flops 13107200 | bytes 10485760 | tf_op jit(solution)/shard_map/norm/pallas_call | solution.py:35
  5.9 1.5 %collective-permute-start.2 = (bf16[2,256,2560]{2,1,0:T(8,128)(2,1)S(1)}, bf16[2,256,2560]{2,1,0:T(8,128)(2,1)S(1)}, u32[]{:S(2)}, u32[]{:S(2)}) collective-permute-start(bf16[2,256,2560]{2,1,0:T(8,128)(2,1)S(1)} %get-tuple-element.30), channel_id=1, source_target_pairs={{0,64},{64,0},{1,65},{65,1},{2,66},{66,2},{3,67},{67,3},{4,68},{68... | collective-permute-start | bytes 7864328 | tf_op jit(solution)/shard_map/ppermute | solution.py:14
  7.3 2.7 %project.4 = (f32[3,128,384]{2,1,0:T(8,128)S(1)}, f32[3,128,384]{2,1,0:T(8,128)S(1)}, bf16[2,2560,384]{2,1,0:T(8,128)(2,1)S(1)}) custom-call(s32[3]{0:T(128)S(1)} %pad_add_fusion.info_ref, bf16[3,2560,384]{2,1,0:T(8,128)(2,1)} %bitcast.9, bf16[2,256,2560]{2,1,0:T(8,128)(2,1)S(1)} %get-tuple-element.27.refs_1_, ...), custom_call_target="tpu_custom_call" | custom-call | flops 1509949440 | bytes 7208960 | tf_op jit(solution)/shard_map/project/pallas_call | solution.py:35
  10.1 0.1 collective-permute-start.4
  10.2 3.3 %project.6 = (f32[3,128,384]{2,1,0:T(8,128)S(1)}, f32[3,128,384]{2,1,0:T(8,128)S(1)}, bf16[1,2560,384]{2,1,0:T(8,128)(2,1)S(1)}) custom-call(s32[3]{0:T(128)S(1)} %pad_add_fusion.info_ref, bf16[3,2560,384]{2,1,0:T(8,128)(2,1)} %bitcast.10, bf16[2,256,2560]{2,1,0:T(8,128)(2,1)S(1)} %get-tuple-element.27.refs_1_, ...), custom_call_target="tpu_custom_call" | custom-call | flops 1509949440 | bytes 7208960 | tf_op jit(solution)/shard_map/project/pallas_call | solution.py:35
  13.5 0.6 collective-permute-start.6
  14.0 0.0 collective-permute-done.2.refs_0_
  14.0 2.4 %project.5 = (f32[3,128,384]{2,1,0:T(8,128)S(1)}, f32[3,128,384]{2,1,0:T(8,128)S(1)}) custom-call(s32[3]{0:T(128)S(1)} %pad_add_fusion.info_ref, bf16[2,256,2560]{2,1,0:T(8,128)(2,1)S(1)} %collective-permute-done.2.refs_0_, bf16[3,2560,384]{2,1,0:T(8,128)(2,1)S(1)} %get-tuple-element.28.refs_2_.refs_1_), custom_call_target="tpu_custom_call" | custom-call | flops 1509949440 | bytes 7208960 | tf_op jit(solution)/shard_map/project/pallas_call | solution.py:35
  16.5 0.1 collective-permute-start.3
  16.6 2.4 %project.7 = (f32[3,128,384]{2,1,0:T(8,128)S(1)}, f32[3,128,384]{2,1,0:T(8,128)S(1)}) custom-call(s32[3]{0:T(128)S(1)} %pad_add_fusion.info_ref, bf16[2,256,2560]{2,1,0:T(8,128)(2,1)S(1)} %collective-permute-done.2.refs_0_, bf16[2,2560,384]{2,1,0:T(8,128)(2,1)S(1)} %get-tuple-element.34.refs_2_.refs_1_, bf16[1,2560,384]{2,1,0:T(8,128)(2,1)S(1)} %get-tuple-element.36.refs_2_), custom_call_target="tpu_custom_call" | custom-call | flops 1509949440 | bytes 7208960 | tf_op jit(solution)/shard_map/project/pallas_call | solution.py:35
  19.0 0.6 collective-permute-start.5
  19.6 0.0 collective-permute-done.4.refs_3_
  19.6 0.0 collective-permute-done.3.refs_1_
  19.6 1.5 %join.2.refs_0_ = bf16[8,704,128]{2,1,0:T(8,128)(2,1)} custom-call(s32[3]{0:T(128)S(1)} %pad_add_fusion.info_ref, f32[3,128,384]{2,1,0:T(8,128)S(1)} %get-tuple-element.29.refs_0_, f32[3,128,384]{2,1,0:T(8,128)S(1)} %collective-permute-done.3.refs_1_, f32[3,128,384]{2,1,0:T(8,128)S(1)} %get-tuple-element.32.refs_2_, ...), custom_call_target="tpu_custom_call" | custom-call | flops 294912 | bytes 2949120 | tf_op jit(solution)/shard_map/join/pallas_call | solution.py:35
  21.1 0.0 collective-permute-done.6.refs_4_
  21.1 0.1 collective-permute-done.5.refs_2_
  21.2 1.5 %join.3 = bf16[8,704,128]{2,1,0:T(8,128)(2,1)} custom-call(s32[3]{0:T(128)S(1)} %pad_add_fusion.info_ref, bf16[8,704,128]{2,1,0:T(8,128)(2,1)} %join.2.refs_0_, f32[3,128,384]{2,1,0:T(8,128)S(1)} %get-tuple-element.35.refs_1_, f32[3,128,384]{2,1,0:T(8,128)S(1)} %collective-permute-done.5.refs_2_, ...), custom_call_target="tpu_custom_call", output_to_operand_aliasing={{}: (1, {})} | custom-call | flops 294912 | bytes 2949120 | tf_op jit(solution)/shard_map/join/pallas_call | solution.py:35
  22.7 6.1 %all-to-all-start = ((bf16[8,704,128]{2,1,0:T(8,128)(2,1)}), bf16[8,704,128]{2,1,0:T(8,128)(2,1)S(1)}, u32[]{:S(2)}, u32[]{:S(2)}) async-start(bf16[8,704,128]{2,1,0:T(8,128)(2,1)} %join.3), calls=%async_computation | async-start | bytes 2883584 | tf_op jit(solution)/shard_map/all_to_all | solution.py:18
  28.8 0.6 collective-permute-start
  29.4 0.1 collective-permute-start.1
  29.5 18.7 %all-to-all-done.refs_2_.refs_3_ = bf16[8,704,128]{2,1,0:T(8,128)(2,1)S(1)} async-done(((bf16[8,704,128]{2,1,0:T(8,128)(2,1)}), bf16[8,704,128]{2,1,0:T(8,128)(2,1)S(1)}, u32[]{:S(2)}, u32[]{:S(2)}) %all-to-all-start) | async-done | bytes 1441824 | tf_op jit(solution)/shard_map/all_to_all | solution.py:18
  48.2 1.5 %collective-permute-start.7 = (bf16[8,704,128]{2,1,0:T(8,128)(2,1)S(1)}, bf16[8,704,128]{2,1,0:T(8,128)(2,1)S(1)}, u32[]{:S(2)}, u32[]{:S(2)}) collective-permute-start(bf16[8,704,128]{2,1,0:T(8,128)(2,1)S(1)} %all-to-all-done.refs_2_.refs_3_), channel_id=1, source_target_pairs={{0,64},{64,0},{1,65},{65,1},{2,66},{66,2},{3,67},{67,3},{4,68},{68... | collective-permute-start | bytes 4325384 | tf_op jit(solution)/shard_map/ppermute | solution.py:14
  49.7 2.8 %attend.2 = (bf16[384,2560]{1,0:T(8,128)(2,1)S(1)}, bf16[384,2560]{1,0:T(8,128)(2,1)S(1)}, f32[1536,128]{1,0:T(8,128)S(1)}, f32[1536,128]{1,0:T(8,128)S(1)}, f32[1536,128]{1,0:T(8,128)S(1)}) custom-call(s32[3]{0:T(128)S(1)} %pad_add_fusion.info_ref, bf16[384,2560]{1,0:T(8,128)(2,1)} %refs_0_.1, bf16[384,2560]{1,0:T(8,128)(2,1)} %refs_1_.1, ...), custom_call_target="tpu_custom_call" | custom-call | flops 805306368 | bytes 1310720 | tf_op jit(solution)/shard_map/attend/pallas_call | solution.py:35
  52.5 0.0 collective-permute-done.refs_0_
  52.5 0.0 collective-permute-done.1.refs_1_
  52.5 0.0 collective-permute-done.7.refs_3_
  52.5 3.3 %attend.3 = (bf16[384,2560]{1,0:T(8,128)(2,1)S(1)}, bf16[384,2560]{1,0:T(8,128)(2,1)S(1)}, bf16[8,192,128]{2,1,0:T(8,128)(2,1)S(1)}, f32[8,128]{1,0:T(8,128)S(1)}) custom-call(s32[3]{0:T(128)S(1)} %pad_add_fusion.info_ref, bf16[384,2560]{1,0:T(8,128)(2,1)S(1)} %collective-permute-done.refs_0_, bf16[384,2560]{1,0:T(8,128)(2,1)} %collective-permute-done.1.refs_1_, ...), custom_call_target="tpu_custom_call" | custom-call | flops 805306368 | bytes 1310720 | tf_op jit(solution)/shard_map/attend/pallas_call | solution.py:35
  55.9 10.7 %all_to_all.15.attn_ref = bf16[8,192,128]{2,1,0:T(8,128)(2,1)S(1)} all-to-all(bf16[8,192,128]{2,1,0:T(8,128)(2,1)S(1)} %get-tuple-element.44), channel_id=1, replica_groups=mesh['dp'=2,'ctx'=8,'tp'=8] {'ctx'}, dimensions={0} | all-to-all | bytes 786432 | tf_op jit(solution)/shard_map/all_to_all | solution.py:18
  66.5 2.8 %expand.1 = bf16[16,128,640]{2,1,0:T(8,128)(2,1)S(1)} custom-call(s32[3]{0:T(128)S(1)} %pad_add_fusion.info_ref, bf16[8,192,128]{2,1,0:T(8,128)(2,1)S(1)} %all_to_all.15.attn_ref, bf16[384,2560]{1,0:T(8,128)(2,1)S(1)} %get-tuple-element.45.refs_0_, bf16[384,2560]{1,0:T(8,128)(2,1)S(1)} %get-tuple-element.46.refs_1_, ...), custom_call_target="tpu_custom_call" | custom-call | flops 2013265920 | bytes 7864320 | tf_op jit(solution)/shard_map/expand/pallas_call | solution.py:35
  69.3 42.4 %all_to_all.16.block_ref = bf16[16,128,640]{2,1,0:T(8,128)(2,1)S(1)} all-to-all(bf16[16,128,640]{2,1,0:T(8,128)(2,1)S(1)} %expand.1), channel_id=1, replica_groups=mesh['dp'=2,'ctx'=8,'tp'=8] {'dp','tp'}, dimensions={0} | all-to-all | bytes 5242880 | tf_op jit(solution)/shard_map/all_to_all | solution.py:18
  111.7 1.1 collect.1
Async XLA Ops:
  5.9 8.2 %collective-permute-start.2 = (bf16[2,256,2560]{2,1,0:T(8,128)(2,1)S(1)}, bf16[2,256,2560]{2,1,0:T(8,128)(2,1)S(1)}, u32[]{:S(2)}, u32[]{:S(2)}) collective-permute-start(bf16[2,256,2560]{2,1,0:T(8,128)(2,1)S(1)} %get-tuple-element.30), channel_id=1, source_target_pairs={{0,64},{64,0},{1,65},{65,1},{2,66},{66,2},{3,67},{67,3},{4,68},{68... | collective-permute-start | bytes 7864328 | tf_op jit(solution)/shard_map/ppermute | solution.py:14
  10.1 9.5 %collective-permute-start.4 = (f32[3,128,384]{2,1,0:T(8,128)S(1)}, f32[3,128,384]{2,1,0:T(8,128)S(1)}, u32[]{:S(2)}, u32[]{:S(2)}) collective-permute-start(f32[3,128,384]{2,1,0:T(8,128)S(1)} %get-tuple-element.33), channel_id=1, source_target_pairs={{0,64},{64,0},{1,65},{65,1},{2,66},{66,2},{3,67},{67,3},{4,68},{68... | collective-permute-start | bytes 1769480 | tf_op jit(solution)/shard_map/ppermute | solution.py:14
  13.5 7.6 %collective-permute-start.6 = (f32[3,128,384]{2,1,0:T(8,128)S(1)}, f32[3,128,384]{2,1,0:T(8,128)S(1)}, u32[]{:S(2)}, u32[]{:S(2)}) collective-permute-start(f32[3,128,384]{2,1,0:T(8,128)S(1)} %get-tuple-element.39), channel_id=1, source_target_pairs={{0,64},{64,0},{1,65},{65,1},{2,66},{66,2},{3,67},{67,3},{4,68},{68... | collective-permute-start | bytes 1769480 | tf_op jit(solution)/shard_map/ppermute | solution.py:14
  16.5 3.1 %collective-permute-start.3 = (f32[3,128,384]{2,1,0:T(8,128)S(1)}, f32[3,128,384]{2,1,0:T(8,128)S(1)}, u32[]{:S(2)}, u32[]{:S(2)}) collective-permute-start(f32[3,128,384]{2,1,0:T(8,128)S(1)} %get-tuple-element.31), channel_id=1, source_target_pairs={{0,64},{64,0},{1,65},{65,1},{2,66},{66,2},{3,67},{67,3},{4,68},{68... | collective-permute-start | bytes 1769480 | tf_op jit(solution)/shard_map/ppermute | solution.py:14
  19.0 2.2 %collective-permute-start.5 = (f32[3,128,384]{2,1,0:T(8,128)S(1)}, f32[3,128,384]{2,1,0:T(8,128)S(1)}, u32[]{:S(2)}, u32[]{:S(2)}) collective-permute-start(f32[3,128,384]{2,1,0:T(8,128)S(1)} %get-tuple-element.37), channel_id=1, source_target_pairs={{0,64},{64,0},{1,65},{65,1},{2,66},{66,2},{3,67},{67,3},{4,68},{68... | collective-permute-start | bytes 1769480 | tf_op jit(solution)/shard_map/ppermute | solution.py:14
  22.7 25.5 %all-to-all-start = ((bf16[8,704,128]{2,1,0:T(8,128)(2,1)}), bf16[8,704,128]{2,1,0:T(8,128)(2,1)S(1)}, u32[]{:S(2)}, u32[]{:S(2)}) async-start(bf16[8,704,128]{2,1,0:T(8,128)(2,1)} %join.3), calls=%async_computation | async-start | bytes 2883584 | tf_op jit(solution)/shard_map/all_to_all | solution.py:18
  28.8 23.7 %collective-permute-start = (bf16[384,2560]{1,0:T(8,128)(2,1)}, bf16[384,2560]{1,0:T(8,128)(2,1)S(1)}, u32[]{:S(2)}, u32[]{:S(2)}) collective-permute-start(bf16[384,2560]{1,0:T(8,128)(2,1)} %refs_0_.1), channel_id=1, source_target_pairs={{0,64},{64,0},{1,65},{65,1},{2,66},{66,2},{3,67},{67,3},{4,68},{68... | collective-permute-start | bytes 5898248 | tf_op jit(solution)/shard_map/ppermute | solution.py:14
  29.4 23.1 %collective-permute-start.1 = (bf16[384,2560]{1,0:T(8,128)(2,1)}, bf16[384,2560]{1,0:T(8,128)(2,1)}, u32[]{:S(2)}, u32[]{:S(2)}) collective-permute-start(bf16[384,2560]{1,0:T(8,128)(2,1)} %refs_1_.1), channel_id=1, source_target_pairs={{0,64},{64,0},{1,65},{65,1},{2,66},{66,2},{3,67},{67,3},{4,68},{68... | collective-permute-start | bytes 5898248 | tf_op jit(solution)/shard_map/ppermute | solution.py:14
  48.2 4.4 %collective-permute-start.7 = (bf16[8,704,128]{2,1,0:T(8,128)(2,1)S(1)}, bf16[8,704,128]{2,1,0:T(8,128)(2,1)S(1)}, u32[]{:S(2)}, u32[]{:S(2)}) collective-permute-start(bf16[8,704,128]{2,1,0:T(8,128)(2,1)S(1)} %all-to-all-done.refs_2_.refs_3_), channel_id=1, source_target_pairs={{0,64},{64,0},{1,65},{65,1},{2,66},{66,2},{3,67},{67,3},{4,68},{68... | collective-permute-start | bytes 4325384 | tf_op jit(solution)/shard_map/ppermute | solution.py:14
where the time goes:
time: 113 us
  blocking collectives  53.1 us (47%)
  Pallas kernels  28.9 us (26%)
  waiting for transfers between devices  18.8 us (17%)
  starting transfers between devices  11.1 us (10%)
    all_to_all x2, blocking collectives, exchange(): return lax.all_to_all(value, axes, 0, 0, tiled=True)  53.1 us
    pallas_call x10, Pallas kernels, kernel(): pl.pallas_call(body, in_specs=[SCALAR] + [ANYWHERE] * len(far) + [NEAR] *...  27.8 us
    all_to_all x1, waiting for transfers between devices, exchange(): return lax.all_to_all(value, axes, 0, 0, tiled=True)  18.7 us
    all_to_all x1, starting transfers between devices, exchange(): return lax.all_to_all(value, axes, 0, 0, tiled=True)  6.06 us
    ppermute x8, starting transfers between devices, swapped(): return lax.ppermute(value, 'dp', [(0, 1), (1, 0)])  5.05 us
  transfers between devices with their start and end apart: 9, of which 2 were waited for; matrix products, arithmetic and copies ran while one was open for 0% of the time, Pallas kernels for 13%

commit v1 on v0

--- a/solution.py
+++ b/solution.py
@@ -8,6 +8,14 @@
 
 HD = 128
 MIB = 1024 * 1024
+XH, Y = 2, 4
+
+
+def over_tp(value, xh, y):
+    pairs = [
+        (e * Y + f, (e + xh) % XH * Y + (f + y) % Y) for e in range(XH) for f in range(Y)
+    ]
+    return lax.ppermute(value, "tp", pairs)
 
 
 def swapped(value):
@@ -31,7 +39,7 @@
 ANYWHERE = pl.BlockSpec(memory_space=pl.ANY)
 
 
-def kernel(body, name, info, far, near, made, mib, flops, size, exps=0, scratch=(), loose=(), aliases=None):
+def kernel(body, name, info, far, near, made, mib, flops, size, exps=0, scratch=(), loose=()):
     return pl.pallas_call(
         body,
         in_specs=[SCALAR] + [ANYWHERE] * len(far) + [NEAR] * len(near),
@@ -39,7 +47,6 @@
         out_shape=[pltpu.VMEM(shape, dtype) for shape, dtype in made]
         + [pltpu.HBM(shape, dtype) for shape, dtype in loose],
         scratch_shapes=list(scratch),
-        input_output_aliases=aliases or {},
         compiler_params=pltpu.CompilerParams(vmem_limit_bytes=mib * MIB),
         cost_estimate=pl.CostEstimate(flops=flops, bytes_accessed=size, transcendentals=exps),
         name=name,
@@ -52,7 +59,7 @@
 
 BF16, F32 = jnp.bfloat16, jnp.float32
 
-AT_CORE, AT_CTX, AT_STEP = range(3)
+AT_CORE, AT_CTX, AT_STEP, AT_XH, AT_Y = range(5)
 
 
 def noise_level(info_ref):
@@ -158,12 +165,13 @@
     )
 
 
-def project(info, model, a, weights, hold=None, fetch=None):
+def project(info, model, a, weights, hold=None, fetch=None, halves=(0, 1)):
     _, tokens, depth = a.shape
     panel = weights[0].shape[-1]
     kinds = 3
-    shape = ((kinds, tokens // 2, panel), F32)
-    made = (shape, shape)
+    half = tokens // 2
+    lines = slice(halves[0] * half, (halves[-1] + 1) * half)
+    made = (((kinds, half, panel), F32),) * len(halves)
     if hold is not None:
         made += (((kinds - 1, depth, panel), BF16),)
     if fetch is not None:
@@ -173,7 +181,8 @@
     def body(info_ref, *refs):
         sources, rest = refs[: len(far)], refs[len(far) :]
         a_ref, *w_refs = rest[: 1 + len(weights)]
-        top_ref, bottom_ref, *brought, sem = rest[1 + len(weights) :]
+        *outs, sem = rest[1 + len(weights) :]
+        outs, brought = outs[: len(halves)], outs[len(halves) :]
         first = 0 if fetch is None else kinds - 1
         copies = [
             pltpu.make_async_copy(sources[0].at[first + j], brought[0].at[j], sem.at[j])
@@ -184,12 +193,12 @@
 
         def product(slices, j):
             value = jnp.dot(
-                a_ref[model], jnp.concatenate(slices, axis=1), preferred_element_type=F32
+                a_ref[model, lines], jnp.concatenate(slices, axis=1), preferred_element_type=F32
             )
             for n in range(len(slices)):
                 part = value[:, n * panel : (n + 1) * panel]
-                top_ref[j + n] = part[: tokens // 2]
-                bottom_ref[j + n] = part[tokens // 2 :]
+                for i, out in enumerate(outs):
+                    out[j + n] = part[i * half : (i + 1) * half]
 
         product([w[j] for w in w_refs for j in range(w.shape[0])], 0)
         for copy in copies:
@@ -205,7 +214,7 @@
         (a, *weights),
         made,
         8,
-        2 * tokens * depth * panel * kinds,
+        2 * half * len(halves) * depth * panel * kinds,
         2 * depth * (tokens + panel * kinds),
         scratch=(pltpu.SemaphoreType.DMA((kinds,)),),
     )
@@ -214,18 +223,35 @@
 UNITS = 8
 
 
-def join(info, model, parts, blocks=None):
+def join(info, parts, done=None):
     _, rows, panel = parts[0].shape
     half = rows // 2
     shape = (UNITS, 5 * rows + half, HD)
+    part = (4, *shape[1:])
 
     def body(info_ref, *refs):
-        target, out, sem = refs[-3:]
-        inputs = refs[-3 - len(parts) : -3]
+        inputs, rest = refs[: len(parts)], refs[len(parts) :]
         copies = []
+
+        def leave(source, model, which):
+            clip = info_ref[AT_CORE] if which == 0 else 1 - info_ref[AT_CORE]
+            copies.append(
+                pltpu.make_async_copy(
+                    source.at[pl.ds(2 * which, 2)],
+                    target.at[pl.ds(4 * model + 2 * clip, 2)],
+                    sem.at[2 * model + which],
+                )
+            )
+            copies[-1].start()
+
+        if done is None:
+            (out,) = rest
+        else:
+            teacher, target, out, sem = rest
+            leave(teacher, 0, 0)
+            leave(teacher, 0, 1)
         for which in range(2):
             left, right = inputs[2 * which : 2 * which + 2]
-            clip = info_ref[AT_CORE] if which == 0 else 1 - info_ref[AT_CORE]
             for kind, base in ((1, 0), (2, 2 * rows), (0, 4 * rows)):
                 value = (left[kind] + right[kind]).astype(BF16)
                 for j in range(2):
@@ -235,14 +261,8 @@
                     if kind == 0:
                         middle = middle[j * half : (j + 1) * half]
                     out[block, base + rows : base + rows + middle.shape[0]] = middle
-            copies.append(
-                pltpu.make_async_copy(
-                    out.at[pl.ds(2 * which, 2)],
-                    target.at[pl.ds(4 * model + 2 * clip, 2)],
-                    sem.at[which],
-                )
-            )
-            copies[-1].start()
+            if done is not None:
+                leave(out, 1, which)
         for copy in copies:
             copy.wait()
 
@@ -250,15 +270,16 @@
         body,
         "join",
         info,
-        () if blocks is None else (blocks,),
-        parts,
         (),
+        parts if done is None else (*parts, done),
+        ((part, BF16),) if done is None else (),
         8,
         6 * rows * panel,
         60 * rows * panel,
-        scratch=(pltpu.VMEM((4, *shape[1:]), BF16), pltpu.SemaphoreType.DMA((2,))),
-        loose=((shape, BF16),),
-        aliases={} if blocks is None else {1: 0},
+        scratch=()
+        if done is None
+        else (pltpu.VMEM(part, BF16), pltpu.SemaphoreType.DMA((4,))),
+        loose=() if done is None else ((shape, BF16),),
     )[0]
 
 
@@ -359,11 +380,10 @@
     half = size // 3
     rows, panel = 2 * half, 3 * HD
     columns = mine[0].shape[1]
-    part = columns // 4
-    shape = ((2 * UNITS, rows, part), BF16)
+    part = columns // Y
 
     def body(info_ref, attn_ref, *refs):
-        weights, (out, left) = refs[:4], refs[4:]
+        weights, (to_x, *to_y, own_y, own_x, left) = refs[:4], refs[4:]
         for unit in range(UNITS):
             model, clip, j = unit // 4, unit // 2 % 2, unit % 2
             line, lane = clip * rows, model * panel
@@ -375,53 +395,118 @@
         for i in range(0, 8, 2):
             place = slice(i % 4 * part, (i % 4 + 2) * part)
             right = jnp.concatenate([w[:, place] for w in weights[i // 4 * 2 : i // 4 * 2 + 2]])
-            value = jnp.dot(left[...], right, preferred_element_type=F32).astype(BF16)
-            way = info_ref[AT_CORE] if i < 4 else 1 - info_ref[AT_CORE]
-            for clip in range(2):
-                block = clip * UNITS + way * 4 + i % 4
-                for n in range(2):
-                    out[block + n] = value[
-                        clip * rows : (clip + 1) * rows, n * part : (n + 1) * part
-                    ]
-
+            value = jnp.dot(left[...], right, preferred_element_type=F32)
+            xh = info_ref[AT_CORE] if i < 4 else 1 - info_ref[AT_CORE]
+            here = xh == info_ref[AT_XH]
+            for n in range(2):
+                y = i % 4 + n
+                shift = lax.rem(y - info_ref[AT_Y] + Y, Y)
+                first = value[:rows, n * part : (n + 1) * part]
+                second = value[rows:, n * part : (n + 1) * part]
+                for f, target in enumerate((own_y, *to_y)):
+
+                    @pl.when(shift == f)
+                    def _():
+                        target[xh] = first.astype(target.dtype)
+
+                @pl.when(here)
+                def _():
+                    own_x[y] = second
+
+                @pl.when(jnp.logical_not(here))
+                def _():
+                    to_x[y] = second.astype(BF16)
+
+    by_x, by_y = (Y, rows, part), (XH, rows, part)
     return kernel(
         body,
         "expand",
         info,
         (),
         (attn, *mine, *other),
-        (shape,),
+        ((by_x, BF16), *[(by_y, BF16)] * (Y - 1), (by_y, F32), (by_x, F32)),
         12,
         16 * rows * panel * columns,
         8 * panel * columns,
         scratch=(pltpu.VMEM((2 * rows, 2 * panel), BF16),),
-    )[0]
-
-
-def collect(level, blocks):
-    _, rows, width = blocks.shape
-
-    def body(level_ref, block_ref, out_ref):
+    )
+
+
+def turn(info, own_y, own_x, from_x, from_y):
+    _, rows, part = own_y.shape
+
+    def body(info_ref, own_y_ref, own_x_ref, from_x_ref, *refs):
+        from_y_refs, (keep_a, keep_b, to_x, *to_y) = refs[: Y - 1], refs[Y - 1 :]
+        xh, y = info_ref[AT_XH], info_ref[AT_Y]
+        for out, place in ((to_x, 1 - xh), (keep_a, xh)):
+            total = own_y_ref[place]
+            for ref in from_y_refs:
+                total = total + ref[place].astype(F32)
+            out[...] = total.astype(out.dtype)
+        for f, out in enumerate((keep_b, *to_y)):
+            place = lax.rem(y + f, Y)
+            total = own_x_ref[place] + from_x_ref[place].astype(F32)
+            out[...] = total.astype(out.dtype)
+
+    shape = (rows, part)
+    return kernel(
+        body,
+        "turn",
+        info,
+        (),
+        (own_y, own_x, from_x, *from_y),
+        ((shape, F32), (shape, F32), *[(shape, BF16)] * Y),
+        8,
+        12 * rows * part,
+        60 * rows * part,
+    )
+
+
+def collect(info, keep_a, keep_b, from_x, from_y):
+    shape = keep_a.shape
+
+    def body(info_ref, a_ref, b_ref, x_ref, *refs):
+        y_refs, (own, away) = refs[: Y - 1], refs[Y - 1 :]
+        for core, (first, second) in enumerate(((own, away), (away, own))):
+
+            @pl.when(info_ref[AT_CORE] == core)
+            def _():
+                first[...] = a_ref[...] + x_ref[...].astype(F32)
+                total = b_ref[...]
+                for ref in y_refs:
+                    total = total + ref[...].astype(F32)
+                second[...] = total
+
+    return kernel(
+        body,
+        "collect",
+        info,
+        (),
+        (keep_a, keep_b, from_x, *from_y),
+        ((shape, F32), (shape, F32)),
+        4,
+        4 * shape[0] * shape[1],
+        30 * shape[0] * shape[1],
+    )
+
+
+def scale(info, level, own, came):
+    rows, width = own.shape
+
+    def body(info_ref, level_ref, own_ref, came_ref, out_ref):
         level = level_ref[:1, :1]
-        step = 32
-        for core in range(2):
-            for line in range(0, rows, step):
-                place = slice(line, line + step)
-                total = block_ref[core * UNITS, place].astype(F32)
-                for tp in range(1, UNITS):
-                    total = total + block_ref[core * UNITS + tp, place].astype(F32)
-                out_ref[core * rows + line : core * rows + line + step] = (level * total).astype(
-                    BF16
-                )
+        for source, part in ((own_ref, info_ref[AT_CORE]), (came_ref, 1 - info_ref[AT_CORE])):
+            place = pl.ds(pl.multiple_of(part * rows, rows), rows)
+            out_ref[place, :] = (level * source[...]).astype(BF16)
 
     return pl.pallas_call(
         body,
-        in_specs=[NEAR, NEAR],
+        in_specs=[SCALAR, NEAR, NEAR, NEAR],
         out_specs=NEAR,
         out_shape=jax.ShapeDtypeStruct((2 * rows, width), BF16),
-        compiler_params=pltpu.CompilerParams(vmem_limit_bytes=8 * MIB),
-        name="collect",
-    )(in_vmem(level), in_vmem(blocks))
+        compiler_params=pltpu.CompilerParams(vmem_limit_bytes=4 * MIB),
+        name="scale",
+    )(info, in_vmem(level), in_vmem(own), in_vmem(came))
 
 
 def local(
@@ -435,7 +520,8 @@
     teacher_out,
     critic_out,
 ):
-    places = [lax.axis_index("dp"), lax.axis_index("ctx"), timestep[0]]
+    tp = lax.axis_index("tp")
+    places = [lax.axis_index("dp"), lax.axis_index("ctx"), timestep[0], tp // Y, tp % Y]
     info = lax.optimization_barrier(jnp.stack(places).astype(jnp.int32))
 
     weights = [jnp.transpose(w, (1, 0, 2)) for w in (teacher_qkv, critic_qkv)]
@@ -448,17 +534,23 @@
     other = [swapped(out) for out in outs]
     *own_c, last_c = project(info, 1, keep, (most_c,), fetch=weights[1])
     cross_t = project(info, 0, came, (weights_t,))
-    cross_c = project(info, 1, came, (most_c, last_c))
+    cross_c = [project(info, 1, came, (most_c, last_c), halves=(i,))[0] for i in range(2)]
     blocks = None
-    for m, (own, cross) in enumerate(((own_t, cross_t), (own_c, cross_c))):
+    for own, cross in ((own_t, cross_t), (own_c, cross_c)):
         parts = (own[0], swapped(cross[0]), cross[1], swapped(own[1]))
-        blocks = join(info, m, parts, blocks)
+        blocks = join(info, parts, blocks)
 
     block = exchange(blocks, "ctx")
     *mine, peak, total, summed = attend(info, block, block, [in_hbm(out) for out in outs])
     *other, attn, level = attend(info, block, swapped(block), other, (peak, total, summed))
-    sums = expand(info, exchange(attn, "ctx"), mine, other)
-    return collect(level, exchange(sums, ("dp", "tp")))[None]
+    to_x, *to_y, own_y, own_x = expand(info, exchange(attn, "ctx"), mine, other)
+    from_x = over_tp(to_x, 1, 0)
+    from_y = [over_tp(value, 0, f) for f, value in enumerate(to_y, 1)]
+    keep_a, keep_b, to_x, *to_y = turn(info, own_y, own_x, from_x, from_y)
+    from_x = over_tp(to_x, 1, 0)
+    from_y = [over_tp(value, 0, f) for f, value in enumerate(to_y, 1)]
+    own, away = collect(info, keep_a, keep_b, from_x, from_y)
+    return scale(info, level, own, swapped(away))[None]
 
 
 def solution(mesh):

time: 113 us -> 109 us (0.965)
  blocking collectives: 53.1 us -> 10.7 us
  waiting for transfers between devices: 18.8 us -> 39.7 us
  starting transfers between devices: 11.1 us -> 25.4 us
  Pallas kernels: 28.9 us -> 32.1 us
    all_to_all x2 -> x1, blocking collectives: 53.1 us -> 10.7 us  [exchange(): return lax.all_to_all(value, axes, 0, 0, tiled=True)]
    ppermute x0 -> x8, waiting for transfers between devices: none -> 19.1 us  [over_tp(): return lax.ppermute(value, 'tp', pairs)]
    ppermute x0 -> x8, starting transfers between devices: none -> 13.1 us  [over_tp(): return lax.ppermute(value, 'tp', pairs)]
    pallas_call x10 -> x13, Pallas kernels: 27.8 us -> 30.7 us  [kernel(): pl.pallas_call(body, in_specs=[SCALAR] + [ANYWHERE] * len(far) + [NEAR] *...]
    ppermute x8 -> x9, waiting for transfers between devices: 0.16 us -> 1.31 us  [swapped(): return lax.ppermute(value, 'dp', [(0, 1), (1, 0)])]
    ppermute x8 -> x9, starting transfers between devices: 5.05 us -> 6.19 us  [swapped(): return lax.ppermute(value, 'dp', [(0, 1), (1, 0)])]
  transfers between devices with their start and end apart: 9 -> 18, of which waited for: 2 -> 6; matrix products, arithmetic and copies ran while one was open for 0% -> 0% of each run, Pallas kernels for 13% -> 14%
where the time goes in v1:
time: 109 us
  waiting for transfers between devices  39.7 us (36%)
  Pallas kernels  32.1 us (29%)
  starting transfers between devices  25.4 us (23%)
  blocking collectives  10.7 us (10%)
    pallas_call x13, Pallas kernels, kernel(): pl.pallas_call(body, in_specs=[SCALAR] + [ANYWHERE] * len(far) + [NEAR] *...  30.7 us
    all_to_all x1, waiting for transfers between devices, exchange(): return lax.all_to_all(value, axes, 0, 0, tiled=True)  19.3 us
    ppermute x8, waiting for transfers between devices, over_tp(): return lax.ppermute(value, 'tp', pairs)  19.1 us
    ppermute x8, starting transfers between devices, over_tp(): return lax.ppermute(value, 'tp', pairs)  13.1 us
    all_to_all x1, blocking collectives, exchange(): return lax.all_to_all(value, axes, 0, 0, tiled=True)  10.7 us
    ppermute x9, starting transfers between devices, swapped(): return lax.ppermute(value, 'dp', [(0, 1), (1, 0)])  6.19 us
    all_to_all x1, starting transfers between devices, exchange(): return lax.all_to_all(value, axes, 0, 0, tiled=True)  6.06 us
  transfers between devices with their start and end apart: 18, of which 6 were waited for; matrix products, arithmetic and copies ran while one was open for 0% of the time, Pallas kernels for 14%

profile of v1, /device:TPU:1, one launch (start us, length us, event | category | flops | bytes accessed | tf_op | source)
XLA Modules:
  0.0 108.7 jit_solution(18079292256686378453)
XLA Ops:
  0.7 0.1 stack.19.info_ref
  0.7 5.1 %norm.1 = (bf16[2,256,2560]{2,1,0:T(8,128)(2,1)S(1)}, bf16[2,256,2560]{2,1,0:T(8,128)(2,1)S(1)}, bf16[3,2560,384]{2,1,0:T(8,128)(2,1)S(1)}) custom-call(s32[5]{0:T(128)S(1)} %stack.19.info_ref, bf16[256,5120]{1,0:T(8,128)(2,1)} %bitcast.14, bf16[256,5120]{1,0:T(8,128)(2,1)} %bitcast.15, f32[40,128]{1,0:T(8,128)} %bitcast.16, f32[40,128]{1,0:T(8,128)} %bitcast.17, ...), custom_call_target="tpu_custom_call" | custom-call | flops 13107200 | bytes 10485760 | tf_op jit(solution)/shard_map/norm/pallas_call | solution.py:43
  5.9 1.5 %collective-permute-start.2 = (bf16[2,256,2560]{2,1,0:T(8,128)(2,1)S(1)}, bf16[2,256,2560]{2,1,0:T(8,128)(2,1)S(1)}, u32[]{:S(2)}, u32[]{:S(2)}) collective-permute-start(bf16[2,256,2560]{2,1,0:T(8,128)(2,1)S(1)} %get-tuple-element.43), channel_id=1, source_target_pairs={{0,64},{64,0},{1,65},{65,1},{2,66},{66,2},{3,67},{67,3},{4,68},{68... | collective-permute-start | bytes 7864328 | tf_op jit(solution)/shard_map/ppermute | solution.py:22
  7.4 2.7 %project.5 = (f32[3,128,384]{2,1,0:T(8,128)S(1)}, f32[3,128,384]{2,1,0:T(8,128)S(1)}, bf16[2,2560,384]{2,1,0:T(8,128)(2,1)S(1)}) custom-call(s32[5]{0:T(128)S(1)} %stack.19.info_ref, bf16[3,2560,384]{2,1,0:T(8,128)(2,1)} %bitcast.11, bf16[2,256,2560]{2,1,0:T(8,128)(2,1)S(1)} %get-tuple-element.39.refs_1_, ...), custom_call_target="tpu_custom_call" | custom-call | flops 1509949440 | bytes 7208960 | tf_op jit(solution)/shard_map/project/pallas_call | solution.py:43
  10.1 0.1 collective-permute-start.6
  10.2 3.3 %project.6 = (f32[3,128,384]{2,1,0:T(8,128)S(1)}, f32[3,128,384]{2,1,0:T(8,128)S(1)}, bf16[1,2560,384]{2,1,0:T(8,128)(2,1)S(1)}) custom-call(s32[5]{0:T(128)S(1)} %stack.19.info_ref, bf16[3,2560,384]{2,1,0:T(8,128)(2,1)} %bitcast.12, bf16[2,256,2560]{2,1,0:T(8,128)(2,1)S(1)} %get-tuple-element.39.refs_1_, ...), custom_call_target="tpu_custom_call" | custom-call | flops 1509949440 | bytes 7208960 | tf_op jit(solution)/shard_map/project/pallas_call | solution.py:43
  13.5 0.6 collective-permute-start.4
  14.1 0.0 collective-permute-done.2.refs_0_
  14.1 2.4 %project.9 = (f32[3,128,384]{2,1,0:T(8,128)S(1)}, f32[3,128,384]{2,1,0:T(8,128)S(1)}) custom-call(s32[5]{0:T(128)S(1)} %stack.19.info_ref, bf16[2,256,2560]{2,1,0:T(8,128)(2,1)S(1)} %collective-permute-done.2.refs_0_, bf16[3,2560,384]{2,1,0:T(8,128)(2,1)S(1)} %get-tuple-element.40.refs_2_.refs_1_), custom_call_target="tpu_custom_call" | custom-call | flops 1509949440 | bytes 7208960 | tf_op jit(solution)/shard_map/project/pallas_call | solution.py:43
  16.5 0.1 collective-permute-start.5
  16.6 1.6 %project.7 = f32[3,128,384]{2,1,0:T(8,128)S(1)} custom-call(s32[5]{0:T(128)S(1)} %stack.19.info_ref, bf16[2,256,2560]{2,1,0:T(8,128)(2,1)S(1)} %collective-permute-done.2.refs_0_, bf16[2,2560,384]{2,1,0:T(8,128)(2,1)S(1)} %get-tuple-element.41.refs_2_.refs_1_, bf16[1,2560,384]{2,1,0:T(8,128)(2,1)S(1)} %get-tuple-element.44.refs_2_), custom_call_target="tpu_custom_call" | custom-call | flops 754974720 | bytes 7208960 | tf_op jit(solution)/shard_map/project/pallas_call | solution.py:43
  18.2 0.6 collective-permute-start.3
  18.8 1.6 %project.8.refs_2_ = f32[3,128,384]{2,1,0:T(8,128)S(1)} custom-call(s32[5]{0:T(128)S(1)} %stack.19.info_ref, bf16[2,256,2560]{2,1,0:T(8,128)(2,1)S(1)} %collective-permute-done.2.refs_0_, bf16[2,2560,384]{2,1,0:T(8,128)(2,1)S(1)} %get-tuple-element.41.refs_2_.refs_1_, bf16[1,2560,384]{2,1,0:T(8,128)(2,1)S(1)} %get-tuple-element.44.refs_2_), custom_call_target="tpu_custom_call" | custom-call | flops 754974720 | bytes 7208960 | tf_op jit(solution)/shard_map/project/pallas_call | solution.py:43
  20.4 0.0 collective-permute-done.5.refs_1_
  20.4 0.7 join.2.refs_4_
  21.1 0.0 collective-permute-done.3.refs_1_
  21.1 1.7 %join.3 = bf16[8,704,128]{2,1,0:T(8,128)(2,1)} custom-call(s32[5]{0:T(128)S(1)} %stack.19.info_ref, f32[3,128,384]{2,1,0:T(8,128)S(1)} %get-tuple-element.42.refs_0_, f32[3,128,384]{2,1,0:T(8,128)S(1)} %collective-permute-done.3.refs_1_, f32[3,128,384]{2,1,0:T(8,128)S(1)} %project.8.refs_2_, f32[3,128,384]{2,1,0:T(8,128)S(1)} %collective-permute-done.4.refs_3_, ...), custom_call_target="tpu_custom_call" | custom-call | flops 294912 | bytes 2949120 | tf_op jit(solution)/shard_map/join/pallas_call | solution.py:43
  22.8 6.1 %all-to-all-start = ((bf16[8,704,128]{2,1,0:T(8,128)(2,1)}), bf16[8,704,128]{2,1,0:T(8,128)(2,1)S(1)}, u32[]{:S(2)}, u32[]{:S(2)}) async-start(bf16[8,704,128]{2,1,0:T(8,128)(2,1)} %join.3), calls=%async_computation | async-start | bytes 2883584 | tf_op jit(solution)/shard_map/all_to_all | solution.py:26
  28.8 0.3 collective-permute-start
  29.1 0.2 collective-permute-start.1
  29.4 19.3 %all-to-all-done.refs_2_.refs_3_ = bf16[8,704,128]{2,1,0:T(8,128)(2,1)S(1)} async-done(((bf16[8,704,128]{2,1,0:T(8,128)(2,1)}), bf16[8,704,128]{2,1,0:T(8,128)(2,1)S(1)}, u32[]{:S(2)}, u32[]{:S(2)}) %all-to-all-start) | async-done | bytes 1441824 | tf_op jit(solution)/shard_map/all_to_all | solution.py:26
  48.6 1.1 %collective-permute-start.7 = (bf16[8,704,128]{2,1,0:T(8,128)(2,1)S(1)}, bf16[8,704,128]{2,1,0:T(8,128)(2,1)S(1)}, u32[]{:S(2)}, u32[]{:S(2)}) collective-permute-start(bf16[8,704,128]{2,1,0:T(8,128)(2,1)S(1)} %all-to-all-done.refs_2_.refs_3_), channel_id=1, source_target_pairs={{0,64},{64,0},{1,65},{65,1},{2,66},{66,2},{3,67},{67,3},{4,68},{68... | collective-permute-start | bytes 4325384 | tf_op jit(solution)/shard_map/ppermute | solution.py:22
  49.8 2.8 %attend.2 = (bf16[384,2560]{1,0:T(8,128)(2,1)S(1)}, bf16[384,2560]{1,0:T(8,128)(2,1)S(1)}, f32[1536,128]{1,0:T(8,128)S(1)}, f32[1536,128]{1,0:T(8,128)S(1)}, f32[1536,128]{1,0:T(8,128)S(1)}) custom-call(s32[5]{0:T(128)S(1)} %stack.19.info_ref, bf16[384,2560]{1,0:T(8,128)(2,1)} %refs_0_.1, bf16[384,2560]{1,0:T(8,128)(2,1)} %refs_1_.1, ...), custom_call_target="tpu_custom_call" | custom-call | flops 805306368 | bytes 1310720 | tf_op jit(solution)/shard_map/attend/pallas_call | solution.py:43
  52.5 0.0 collective-permute-done.refs_0_
  52.6 0.0 collective-permute-done.1.refs_1_
  52.6 0.0 collective-permute-done.7.refs_3_
  52.6 3.3 %attend.3 = (bf16[384,2560]{1,0:T(8,128)(2,1)S(1)}, bf16[384,2560]{1,0:T(8,128)(2,1)S(1)}, bf16[8,192,128]{2,1,0:T(8,128)(2,1)S(1)}, f32[8,128]{1,0:T(8,128)S(1)}) custom-call(s32[5]{0:T(128)S(1)} %stack.19.info_ref, bf16[384,2560]{1,0:T(8,128)(2,1)S(1)} %collective-permute-done.refs_0_, bf16[384,2560]{1,0:T(8,128)(2,1)} %collective-permute-done.1.refs_1_, ...), custom_call_target="tpu_custom_call" | custom-call | flops 805306368 | bytes 1310720 | tf_op jit(solution)/shard_map/attend/pallas_call | solution.py:43
  55.9 10.7 %all_to_all.10.attn_ref = bf16[8,192,128]{2,1,0:T(8,128)(2,1)S(1)} all-to-all(bf16[8,192,128]{2,1,0:T(8,128)(2,1)S(1)} %get-tuple-element.54), channel_id=1, replica_groups=mesh['dp'=2,'ctx'=8,'tp'=8] {'ctx'}, dimensions={0} | all-to-all | bytes 786432 | tf_op jit(solution)/shard_map/all_to_all | solution.py:26
  66.6 4.1 %expand.1 = (bf16[4,128,640]{2,1,0:T(8,128)(2,1)S(1)}, bf16[2,128,640]{2,1,0:T(8,128)(2,1)S(1)}, bf16[2,128,640]{2,1,0:T(8,128)(2,1)S(1)}, bf16[2,128,640]{2,1,0...) custom-call(s32[5]{0:T(128)S(1)} %stack.19.info_ref, ...), custom_call_target="tpu_custom_call" | custom-call | flops 2013265920 | bytes 7864320 | tf_op jit(solution)/shard_map/expand/pallas_call | solution.py:43
  70.7 2.5 %collective-permute-start.8 = (bf16[4,128,640]{2,1,0:T(8,128)(2,1)S(1)}, bf16[4,128,640]{2,1,0:T(8,128)(2,1)S(1)}, u32[]{:S(2)}, u32[]{:S(2)}) collective-permute-start(bf16[4,128,640]{2,1,0:T(8,128)(2,1)S(1)} %get-tuple-element.61), channel_id=1, source_target_pairs={{0,4},{1,5},{2,6},{3,7},{4,0},{5,1},{6,2},{7,3},{8,12},{9,13},{10,... | collective-permute-start | bytes 1966088 | tf_op jit(solution)/shard_map/ppermute | solution.py:18
  73.2 2.9 %collective-permute-start.10 = (bf16[2,128,640]{2,1,0:T(8,128)(2,1)S(1)}, bf16[2,128,640]{2,1,0:T(8,128)(2,1)S(1)}, u32[]{:S(2)}, u32[]{:S(2)}) collective-permute-start(bf16[2,128,640]{2,1,0:T(8,128)(2,1)S(1)} %get-tuple-element.63), channel_id=1, source_target_pairs={{0,2},{1,3},{2,0},{3,1},{4,6},{5,7},{6,4},{7,5},{8,10},{9,11},{10,... | collective-permute-start | bytes 983048 | tf_op jit(solution)/shard_map/ppermute | solution.py:18
  76.1 0.8 collective-permute-start.11
  76.9 0.7 collective-permute-start.9
  77.6 4.6 %collective-permute-done.10.refs_1_ = bf16[2,128,640]{2,1,0:T(8,128)(2,1)S(1)} collective-permute-done((bf16[2,128,640]{2,1,0:T(8,128)(2,1)S(1)}, bf16[2,128,640]{2,1,0:T(8,128)(2,1)S(1)}, u32[]{:S(2)}, u32[]{:S(2)}) %collective-permute-start.10) | collective-permute-done | bytes 327712 | tf_op jit(solution)/shard_map/ppermute | solution.py:18
  82.1 8.6 %collective-permute-done.11.refs_2_ = bf16[2,128,640]{2,1,0:T(8,128)(2,1)S(1)} collective-permute-done((bf16[2,128,640]{2,1,0:T(8,128)(2,1)S(1)}, bf16[2,128,640]{2,1,0:T(8,128)(2,1)S(1)}, u32[]{:S(2)}, u32[]{:S(2)}) %collective-permute-start.11) | collective-permute-done | bytes 327712 | tf_op jit(solution)/shard_map/ppermute | solution.py:18
  90.7 0.0 collective-permute-done.9.refs_0_
  90.7 0.0 collective-permute-done.8.from_x_ref
  90.7 0.8 turn.1
  91.5 0.6 collective-permute-start.12
  92.1 2.0 %collective-permute-start.13 = (bf16[128,640]{1,0:T(8,128)(2,1)S(1)}, bf16[128,640]{1,0:T(8,128)(2,1)S(1)}, u32[]{:S(2)}, u32[]{:S(2)}) collective-permute-start(bf16[128,640]{1,0:T(8,128)(2,1)S(1)} %get-tuple-element.68), channel_id=1, source_target_pairs={{0,1},{1,2},{2,3},{3,0},{4,5},{5,6},{6,7},{7,4},{8,9},{9,10},{10,1... | collective-permute-start | bytes 491528 | tf_op jit(solution)/shard_map/ppermute | solution.py:18
  94.1 2.6 %collective-permute-start.14 = (bf16[128,640]{1,0:T(8,128)(2,1)S(1)}, bf16[128,640]{1,0:T(8,128)(2,1)S(1)}, u32[]{:S(2)}, u32[]{:S(2)}) collective-permute-start(bf16[128,640]{1,0:T(8,128)(2,1)S(1)} %get-tuple-element.69), channel_id=1, source_target_pairs={{0,2},{1,3},{2,0},{3,1},{4,6},{5,7},{6,4},{7,5},{8,10},{9,11},{10,... | collective-permute-start | bytes 491528 | tf_op jit(solution)/shard_map/ppermute | solution.py:18
  96.7 1.0 collective-permute-start.15
  97.7 0.9 collective-permute-done.13.refs_0_
  98.6 5.0 %collective-permute-done.14.refs_1_ = bf16[128,640]{1,0:T(8,128)(2,1)S(1)} collective-permute-done((bf16[128,640]{1,0:T(8,128)(2,1)S(1)}, bf16[128,640]{1,0:T(8,128)(2,1)S(1)}, u32[]{:S(2)}, u32[]{:S(2)}) %collective-permute-start.14) | collective-permute-done | bytes 163872 | tf_op jit(solution)/shard_map/ppermute | solution.py:18
  103.7 0.6 collect.1
  104.3 1.7 %collective-permute-start.16 = (f32[128,640]{1,0:T(8,128)S(1)}, f32[128,640]{1,0:T(8,128)S(1)}, u32[]{:S(2)}, u32[]{:S(2)}) collective-permute-start(f32[128,640]{1,0:T(8,128)S(1)} %get-tuple-element.72), channel_id=1, source_target_pairs={{0,64},{64,0},{1,65},{65,1},{2,66},{66,2},{3,67},{67,3},{4,68},{68... | collective-permute-start | bytes 983048 | tf_op jit(solution)/shard_map/ppermute | solution.py:22
  106.1 1.3 %collective-permute-done.16.came_ref = f32[128,640]{1,0:T(8,128)S(1)} collective-permute-done((f32[128,640]{1,0:T(8,128)S(1)}, f32[128,640]{1,0:T(8,128)S(1)}, u32[]{:S(2)}, u32[]{:S(2)}) %collective-permute-start.16) | collective-permute-done | bytes 327712 | tf_op jit(solution)/shard_map/ppermute | solution.py:22
  107.3 1.4 %scale.1 = bf16[256,640]{1,0:T(8,128)(2,1)} custom-call(s32[5]{0:T(128)S(1)} %stack.19.info_ref, f32[8,128]{1,0:T(8,128)S(1)} %get-tuple-element.53.level_ref, f32[128,640]{1,0:T(8,128)S(1)} %get-tuple-element.71.own_ref, f32[128,640]{1,0:T(8,128)S(1)} %collective-permute-done.16.came_ref), custom_call_target="tpu_custom_call" | custom-call | tf_op jit(solution)/shard_map/scale/pallas_call | solution.py:502
  (4 shorter events, 0.0 us)
Async XLA Ops:
  5.9 8.2 %collective-permute-start.2 = (bf16[2,256,2560]{2,1,0:T(8,128)(2,1)S(1)}, bf16[2,256,2560]{2,1,0:T(8,128)(2,1)S(1)}, u32[]{:S(2)}, u32[]{:S(2)}) collective-permute-start(bf16[2,256,2560]{2,1,0:T(8,128)(2,1)S(1)} %get-tuple-element.43), channel_id=1, source_target_pairs={{0,64},{64,0},{1,65},{65,1},{2,66},{66,2},{3,67},{67,3},{4,68},{68... | collective-permute-start | bytes 7864328 | tf_op jit(solution)/shard_map/ppermute | solution.py:22
  10.1 10.3 %collective-permute-start.6 = (f32[3,128,384]{2,1,0:T(8,128)S(1)}, f32[3,128,384]{2,1,0:T(8,128)S(1)}, u32[]{:S(2)}, u32[]{:S(2)}) collective-permute-start(f32[3,128,384]{2,1,0:T(8,128)S(1)} %get-tuple-element.49), channel_id=1, source_target_pairs={{0,64},{64,0},{1,65},{65,1},{2,66},{66,2},{3,67},{67,3},{4,68},{68... | collective-permute-start | bytes 1769480 | tf_op jit(solution)/shard_map/ppermute | solution.py:22
  13.5 7.6 %collective-permute-start.4 = (f32[3,128,384]{2,1,0:T(8,128)S(1)}, f32[3,128,384]{2,1,0:T(8,128)S(1)}, u32[]{:S(2)}, u32[]{:S(2)}) collective-permute-start(f32[3,128,384]{2,1,0:T(8,128)S(1)} %get-tuple-element.45), channel_id=1, source_target_pairs={{0,64},{64,0},{1,65},{65,1},{2,66},{66,2},{3,67},{67,3},{4,68},{68... | collective-permute-start | bytes 1769480 | tf_op jit(solution)/shard_map/ppermute | solution.py:22
  16.5 3.9 %collective-permute-start.5 = (f32[3,128,384]{2,1,0:T(8,128)S(1)}, f32[3,128,384]{2,1,0:T(8,128)S(1)}, u32[]{:S(2)}, u32[]{:S(2)}) collective-permute-start(f32[3,128,384]{2,1,0:T(8,128)S(1)} %get-tuple-element.47), channel_id=1, source_target_pairs={{0,64},{64,0},{1,65},{65,1},{2,66},{66,2},{3,67},{67,3},{4,68},{68... | collective-permute-start | bytes 1769480 | tf_op jit(solution)/shard_map/ppermute | solution.py:22
  18.2 2.9 %collective-permute-start.3 = (f32[3,128,384]{2,1,0:T(8,128)S(1)}, f32[3,128,384]{2,1,0:T(8,128)S(1)}, u32[]{:S(2)}, u32[]{:S(2)}) collective-permute-start(f32[3,128,384]{2,1,0:T(8,128)S(1)} %project.7), channel_id=1, source_target_pairs={{0,64},{64,0},{1,65},{65,1},{2,66},{66,2},{3,67},{67,3},{4,68},{68... | collective-permute-start | bytes 1769480 | tf_op jit(solution)/shard_map/ppermute | solution.py:22
  22.8 25.9 %all-to-all-start = ((bf16[8,704,128]{2,1,0:T(8,128)(2,1)}), bf16[8,704,128]{2,1,0:T(8,128)(2,1)S(1)}, u32[]{:S(2)}, u32[]{:S(2)}) async-start(bf16[8,704,128]{2,1,0:T(8,128)(2,1)} %join.3), calls=%async_computation | async-start | bytes 2883584 | tf_op jit(solution)/shard_map/all_to_all | solution.py:26
  28.8 23.7 %collective-permute-start = (bf16[384,2560]{1,0:T(8,128)(2,1)}, bf16[384,2560]{1,0:T(8,128)(2,1)S(1)}, u32[]{:S(2)}, u32[]{:S(2)}) collective-permute-start(bf16[384,2560]{1,0:T(8,128)(2,1)} %refs_0_.1), channel_id=1, source_target_pairs={{0,64},{64,0},{1,65},{65,1},{2,66},{66,2},{3,67},{67,3},{4,68},{68... | collective-permute-start | bytes 5898248 | tf_op jit(solution)/shard_map/ppermute | solution.py:22
  29.1 23.4 %collective-permute-start.1 = (bf16[384,2560]{1,0:T(8,128)(2,1)}, bf16[384,2560]{1,0:T(8,128)(2,1)}, u32[]{:S(2)}, u32[]{:S(2)}) collective-permute-start(bf16[384,2560]{1,0:T(8,128)(2,1)} %refs_1_.1), channel_id=1, source_target_pairs={{0,64},{64,0},{1,65},{65,1},{2,66},{66,2},{3,67},{67,3},{4,68},{68... | collective-permute-start | bytes 5898248 | tf_op jit(solution)/shard_map/ppermute | solution.py:22
  48.6 4.0 %collective-permute-start.7 = (bf16[8,704,128]{2,1,0:T(8,128)(2,1)S(1)}, bf16[8,704,128]{2,1,0:T(8,128)(2,1)S(1)}, u32[]{:S(2)}, u32[]{:S(2)}) collective-permute-start(bf16[8,704,128]{2,1,0:T(8,128)(2,1)S(1)} %all-to-all-done.refs_2_.refs_3_), channel_id=1, source_target_pairs={{0,64},{64,0},{1,65},{65,1},{2,66},{66,2},{3,67},{67,3},{4,68},{68... | collective-permute-start | bytes 4325384 | tf_op jit(solution)/shard_map/ppermute | solution.py:22
  70.7 20.0 %collective-permute-start.8 = (bf16[4,128,640]{2,1,0:T(8,128)(2,1)S(1)}, bf16[4,128,640]{2,1,0:T(8,128)(2,1)S(1)}, u32[]{:S(2)}, u32[]{:S(2)}) collective-permute-start(bf16[4,128,640]{2,1,0:T(8,128)(2,1)S(1)} %get-tuple-element.61), channel_id=1, source_target_pairs={{0,4},{1,5},{2,6},{3,7},{4,0},{5,1},{6,2},{7,3},{8,12},{9,13},{10,... | collective-permute-start | bytes 1966088 | tf_op jit(solution)/shard_map/ppermute | solution.py:18
  73.2 8.9 %collective-permute-start.10 = (bf16[2,128,640]{2,1,0:T(8,128)(2,1)S(1)}, bf16[2,128,640]{2,1,0:T(8,128)(2,1)S(1)}, u32[]{:S(2)}, u32[]{:S(2)}) collective-permute-start(bf16[2,128,640]{2,1,0:T(8,128)(2,1)S(1)} %get-tuple-element.63), channel_id=1, source_target_pairs={{0,2},{1,3},{2,0},{3,1},{4,6},{5,7},{6,4},{7,5},{8,10},{9,11},{10,... | collective-permute-start | bytes 983048 | tf_op jit(solution)/shard_map/ppermute | solution.py:18
  76.1 14.6 %collective-permute-start.11 = (bf16[2,128,640]{2,1,0:T(8,128)(2,1)S(1)}, bf16[2,128,640]{2,1,0:T(8,128)(2,1)S(1)}, u32[]{:S(2)}, u32[]{:S(2)}) collective-permute-start(bf16[2,128,640]{2,1,0:T(8,128)(2,1)S(1)} %get-tuple-element.64), channel_id=1, source_target_pairs={{0,3},{1,0},{2,1},{3,2},{4,7},{5,4},{6,5},{7,6},{8,11},{9,8},{10,9... | collective-permute-start | bytes 983048 | tf_op jit(solution)/shard_map/ppermute | solution.py:18
  76.9 13.8 %collective-permute-start.9 = (bf16[2,128,640]{2,1,0:T(8,128)(2,1)S(1)}, bf16[2,128,640]{2,1,0:T(8,128)(2,1)S(1)}, u32[]{:S(2)}, u32[]{:S(2)}) collective-permute-start(bf16[2,128,640]{2,1,0:T(8,128)(2,1)S(1)} %get-tuple-element.62), channel_id=1, source_target_pairs={{0,1},{1,2},{2,3},{3,0},{4,5},{5,6},{6,7},{7,4},{8,9},{9,10},{10,1... | collective-permute-start | bytes 983048 | tf_op jit(solution)/shard_map/ppermute | solution.py:18
  91.5 6.2 %collective-permute-start.12 = (bf16[128,640]{1,0:T(8,128)(2,1)S(1)}, bf16[128,640]{1,0:T(8,128)(2,1)S(1)}, u32[]{:S(2)}, u32[]{:S(2)}) collective-permute-start(bf16[128,640]{1,0:T(8,128)(2,1)S(1)} %get-tuple-element.67), channel_id=1, source_target_pairs={{0,4},{1,5},{2,6},{3,7},{4,0},{5,1},{6,2},{7,3},{8,12},{9,13},{10,... | collective-permute-start | bytes 491528 | tf_op jit(solution)/shard_map/ppermute | solution.py:18
  92.1 6.5 %collective-permute-start.13 = (bf16[128,640]{1,0:T(8,128)(2,1)S(1)}, bf16[128,640]{1,0:T(8,128)(2,1)S(1)}, u32[]{:S(2)}, u32[]{:S(2)}) collective-permute-start(bf16[128,640]{1,0:T(8,128)(2,1)S(1)} %get-tuple-element.68), channel_id=1, source_target_pairs={{0,1},{1,2},{2,3},{3,0},{4,5},{5,6},{6,7},{7,4},{8,9},{9,10},{10,1... | collective-permute-start | bytes 491528 | tf_op jit(solution)/shard_map/ppermute | solution.py:18
  94.1 9.6 %collective-permute-start.14 = (bf16[128,640]{1,0:T(8,128)(2,1)S(1)}, bf16[128,640]{1,0:T(8,128)(2,1)S(1)}, u32[]{:S(2)}, u32[]{:S(2)}) collective-permute-start(bf16[128,640]{1,0:T(8,128)(2,1)S(1)} %get-tuple-element.69), channel_id=1, source_target_pairs={{0,2},{1,3},{2,0},{3,1},{4,6},{5,7},{6,4},{7,5},{8,10},{9,11},{10,... | collective-permute-start | bytes 491528 | tf_op jit(solution)/shard_map/ppermute | solution.py:18
  96.7 7.0 %collective-permute-start.15 = (bf16[128,640]{1,0:T(8,128)(2,1)S(1)}, bf16[128,640]{1,0:T(8,128)(2,1)S(1)}, u32[]{:S(2)}, u32[]{:S(2)}) collective-permute-start(bf16[128,640]{1,0:T(8,128)(2,1)S(1)} %get-tuple-element.70), channel_id=1, source_target_pairs={{0,3},{1,0},{2,1},{3,2},{4,7},{5,4},{6,5},{7,6},{8,11},{9,8},{10,9... | collective-permute-start | bytes 491528 | tf_op jit(solution)/shard_map/ppermute | solution.py:18
  104.3 3.0 %collective-permute-start.16 = (f32[128,640]{1,0:T(8,128)S(1)}, f32[128,640]{1,0:T(8,128)S(1)}, u32[]{:S(2)}, u32[]{:S(2)}) collective-permute-start(f32[128,640]{1,0:T(8,128)S(1)} %get-tuple-element.72), channel_id=1, source_target_pairs={{0,64},{64,0},{1,65},{65,1},{2,66},{66,2},{3,67},{67,3},{4,68},{68... | collective-permute-start | bytes 983048 | tf_op jit(solution)/shard_map/ppermute | solution.py:22

commit v2 on v1

--- a/solution.py
+++ b/solution.py
@@ -11,11 +11,14 @@
 XH, Y = 2, 4
 
 
-def over_tp(value, xh, y):
+def over_tp(value, xh, y, core=0):
     pairs = [
-        (e * Y + f, (e + xh) % XH * Y + (f + y) % Y) for e in range(XH) for f in range(Y)
+        ((d * XH + e) * Y + f, ((d + core) % 2 * XH + (e + xh) % XH) * Y + (f + y) % Y)
+        for d in range(2)
+        for e in range(XH)
+        for f in range(Y)
     ]
-    return lax.ppermute(value, "tp", pairs)
+    return lax.ppermute(value, ("dp", "tp"), pairs)
 
 
 def swapped(value):
@@ -386,12 +389,16 @@
         weights, (to_x, *to_y, own_y, own_x, left) = refs[:4], refs[4:]
         for unit in range(UNITS):
             model, clip, j = unit // 4, unit // 2 % 2, unit % 2
-            line, lane = clip * rows, model * panel
-            left[line : line + rows, lane + 2 * j * HD : lane + (2 * j + 1) * HD] = attn_ref[
-                unit, :rows
+            lane = model * panel
+            line = lax.rem(clip + info_ref[AT_CORE], 2) * rows
+            left[
+                pl.ds(pl.multiple_of(line, rows), rows),
+                lane + 2 * j * HD : lane + (2 * j + 1) * HD,
+            ] = attn_ref[unit, :rows]
+            line += j * half
+            left[pl.ds(pl.multiple_of(line, half), half), lane + HD : lane + 2 * HD] = attn_ref[
+                unit, rows:
             ]
-            line += j * half
-            left[line : line + half, lane + HD : lane + 2 * HD] = attn_ref[unit, rows:]
         for i in range(0, 8, 2):
             place = slice(i % 4 * part, (i % 4 + 2) * part)
             right = jnp.concatenate([w[:, place] for w in weights[i // 4 * 2 : i // 4 * 2 + 2]])
@@ -462,51 +469,29 @@
     )
 
 
-def collect(info, keep_a, keep_b, from_x, from_y):
-    shape = keep_a.shape
-
-    def body(info_ref, a_ref, b_ref, x_ref, *refs):
-        y_refs, (own, away) = refs[: Y - 1], refs[Y - 1 :]
-        for core, (first, second) in enumerate(((own, away), (away, own))):
-
-            @pl.when(info_ref[AT_CORE] == core)
-            def _():
-                first[...] = a_ref[...] + x_ref[...].astype(F32)
-                total = b_ref[...]
-                for ref in y_refs:
-                    total = total + ref[...].astype(F32)
-                second[...] = total
-
-    return kernel(
-        body,
-        "collect",
-        info,
-        (),
-        (keep_a, keep_b, from_x, *from_y),
-        ((shape, F32), (shape, F32)),
-        4,
-        4 * shape[0] * shape[1],
-        30 * shape[0] * shape[1],
-    )
-
-
-def scale(info, level, own, came):
+def collect(info, level, own, from_x, other, from_y):
     rows, width = own.shape
 
-    def body(info_ref, level_ref, own_ref, came_ref, out_ref):
+    def body(info_ref, level_ref, own_ref, x_ref, other_ref, *refs):
+        y_refs, out_ref = refs[:-1], refs[-1]
         level = level_ref[:1, :1]
-        for source, part in ((own_ref, info_ref[AT_CORE]), (came_ref, 1 - info_ref[AT_CORE])):
+        core = info_ref[AT_CORE]
+        for part, terms in ((core, (own_ref, x_ref)), (1 - core, (other_ref, *y_refs))):
+            total = terms[0][...]
+            for ref in terms[1:]:
+                total = total + ref[...].astype(F32)
             place = pl.ds(pl.multiple_of(part * rows, rows), rows)
-            out_ref[place, :] = (level * source[...]).astype(BF16)
-
+            out_ref[place, :] = (level * total).astype(BF16)
+
+    operands = (level, own, from_x, other, *from_y)
     return pl.pallas_call(
         body,
-        in_specs=[SCALAR, NEAR, NEAR, NEAR],
+        in_specs=[SCALAR] + [NEAR] * len(operands),
         out_specs=NEAR,
         out_shape=jax.ShapeDtypeStruct((2 * rows, width), BF16),
         compiler_params=pltpu.CompilerParams(vmem_limit_bytes=4 * MIB),
-        name="scale",
-    )(info, in_vmem(level), in_vmem(own), in_vmem(came))
+        name="collect",
+    )(info, *[in_vmem(x) for x in operands])
 
 
 def local(
@@ -546,11 +531,10 @@
     to_x, *to_y, own_y, own_x = expand(info, exchange(attn, "ctx"), mine, other)
     from_x = over_tp(to_x, 1, 0)
     from_y = [over_tp(value, 0, f) for f, value in enumerate(to_y, 1)]
-    keep_a, keep_b, to_x, *to_y = turn(info, own_y, own_x, from_x, from_y)
+    own, other, to_x, *to_y = turn(info, own_y, own_x, from_x, from_y)
     from_x = over_tp(to_x, 1, 0)
-    from_y = [over_tp(value, 0, f) for f, value in enumerate(to_y, 1)]
-    own, away = collect(info, keep_a, keep_b, from_x, from_y)
-    return scale(info, level, own, swapped(away))[None]
+    from_y = [over_tp(value, 0, f, 1) for f, value in enumerate(to_y, 1)]
+    return collect(info, level, own, from_x, swapped(other), from_y)[None]
 
 
 def solution(mesh):

time: 109 us -> 107 us (0.982)
    ppermute x9, waiting for transfers between devices: 1.31 us -> 0.05 us  [swapped(): return lax.ppermute(value, 'dp', [(0, 1), (1, 0)])]
    pallas_call x13 -> x12, Pallas kernels: 30.7 us -> 30.1 us  [kernel(): pl.pallas_call(body, in_specs=[SCALAR] + [ANYWHERE] * len(far) + [NEAR] *...]
where the time goes in v2:
time: 107 us
  waiting for transfers between devices  39.1 us (37%)
  Pallas kernels  31.5 us (29%)
  starting transfers between devices  24.7 us (23%)
  blocking collectives  10.7 us (10%)
    pallas_call x12, Pallas kernels, kernel(): pl.pallas_call(body, in_specs=[SCALAR] + [ANYWHERE] * len(far) + [NEAR] *...  30.1 us
    ppermute x8, waiting for transfers between devices, over_tp(): return lax.ppermute(value, ('dp', 'tp'), pairs)  19.8 us
    all_to_all x1, waiting for transfers between devices, exchange(): return lax.all_to_all(value, axes, 0, 0, tiled=True)  19.3 us
    ppermute x8, starting transfers between devices, over_tp(): return lax.ppermute(value, ('dp', 'tp'), pairs)  12.5 us
    all_to_all x1, blocking collectives, exchange(): return lax.all_to_all(value, axes, 0, 0, tiled=True)  10.7 us
    ppermute x9, starting transfers between devices, swapped(): return lax.ppermute(value, 'dp', [(0, 1), (1, 0)])  6.11 us
    all_to_all x1, starting transfers between devices, exchange(): return lax.all_to_all(value, axes, 0, 0, tiled=True)  6.06 us
  transfers between devices with their start and end apart: 18, of which 6 were waited for; matrix products, arithmetic and copies ran while one was open for 0% of the time, Pallas kernels for 14%

profile of v2, /device:TPU:1, one launch (start us, length us, event | category | flops | bytes accessed | tf_op | source)
XLA Modules:
  0.0 106.9 jit_solution(15147001434399377195)
XLA Ops:
  0.7 0.1 stack.19.info_ref
  0.7 5.1 %norm.1 = (bf16[2,256,2560]{2,1,0:T(8,128)(2,1)S(1)}, bf16[2,256,2560]{2,1,0:T(8,128)(2,1)S(1)}, bf16[3,2560,384]{2,1,0:T(8,128)(2,1)S(1)}) custom-call(s32[5]{0:T(128)S(1)} %stack.19.info_ref, bf16[256,5120]{1,0:T(8,128)(2,1)} %bitcast.14, bf16[256,5120]{1,0:T(8,128)(2,1)} %bitcast.15, f32[40,128]{1,0:T(8,128)} %bitcast.16, f32[40,128]{1,0:T(8,128)} %bitcast.17, ...), custom_call_target="tpu_custom_call" | custom-call | flops 13107200 | bytes 10485760 | tf_op jit(solution)/shard_map/norm/pallas_call | solution.py:46
  5.9 1.5 %collective-permute-start.2 = (bf16[2,256,2560]{2,1,0:T(8,128)(2,1)S(1)}, bf16[2,256,2560]{2,1,0:T(8,128)(2,1)S(1)}, u32[]{:S(2)}, u32[]{:S(2)}) collective-permute-start(bf16[2,256,2560]{2,1,0:T(8,128)(2,1)S(1)} %get-tuple-element.41), channel_id=1, source_target_pairs={{0,64},{64,0},{1,65},{65,1},{2,66},{66,2},{3,67},{67,3},{4,68},{68... | collective-permute-start | bytes 7864328 | tf_op jit(solution)/shard_map/ppermute | solution.py:25
  7.4 2.7 %project.5 = (f32[3,128,384]{2,1,0:T(8,128)S(1)}, f32[3,128,384]{2,1,0:T(8,128)S(1)}, bf16[2,2560,384]{2,1,0:T(8,128)(2,1)S(1)}) custom-call(s32[5]{0:T(128)S(1)} %stack.19.info_ref, bf16[3,2560,384]{2,1,0:T(8,128)(2,1)} %bitcast.11, bf16[2,256,2560]{2,1,0:T(8,128)(2,1)S(1)} %get-tuple-element.37.refs_1_, ...), custom_call_target="tpu_custom_call" | custom-call | flops 1509949440 | bytes 7208960 | tf_op jit(solution)/shard_map/project/pallas_call | solution.py:46
  10.1 0.1 collective-permute-start.6
  10.2 3.3 %project.6 = (f32[3,128,384]{2,1,0:T(8,128)S(1)}, f32[3,128,384]{2,1,0:T(8,128)S(1)}, bf16[1,2560,384]{2,1,0:T(8,128)(2,1)S(1)}) custom-call(s32[5]{0:T(128)S(1)} %stack.19.info_ref, bf16[3,2560,384]{2,1,0:T(8,128)(2,1)} %bitcast.12, bf16[2,256,2560]{2,1,0:T(8,128)(2,1)S(1)} %get-tuple-element.37.refs_1_, ...), custom_call_target="tpu_custom_call" | custom-call | flops 1509949440 | bytes 7208960 | tf_op jit(solution)/shard_map/project/pallas_call | solution.py:46
  13.5 0.6 collective-permute-start.4
  14.1 0.0 collective-permute-done.2.refs_0_
  14.1 2.4 %project.9 = (f32[3,128,384]{2,1,0:T(8,128)S(1)}, f32[3,128,384]{2,1,0:T(8,128)S(1)}) custom-call(s32[5]{0:T(128)S(1)} %stack.19.info_ref, bf16[2,256,2560]{2,1,0:T(8,128)(2,1)S(1)} %collective-permute-done.2.refs_0_, bf16[3,2560,384]{2,1,0:T(8,128)(2,1)S(1)} %get-tuple-element.38.refs_2_.refs_1_), custom_call_target="tpu_custom_call" | custom-call | flops 1509949440 | bytes 7208960 | tf_op jit(solution)/shard_map/project/pallas_call | solution.py:46
  16.5 0.1 collective-permute-start.5
  16.6 1.6 %project.7 = f32[3,128,384]{2,1,0:T(8,128)S(1)} custom-call(s32[5]{0:T(128)S(1)} %stack.19.info_ref, bf16[2,256,2560]{2,1,0:T(8,128)(2,1)S(1)} %collective-permute-done.2.refs_0_, bf16[2,2560,384]{2,1,0:T(8,128)(2,1)S(1)} %get-tuple-element.39.refs_2_.refs_1_, bf16[1,2560,384]{2,1,0:T(8,128)(2,1)S(1)} %get-tuple-element.42.refs_2_), custom_call_target="tpu_custom_call" | custom-call | flops 754974720 | bytes 7208960 | tf_op jit(solution)/shard_map/project/pallas_call | solution.py:46
  18.2 0.6 collective-permute-start.3
  18.8 1.6 %project.8.refs_2_ = f32[3,128,384]{2,1,0:T(8,128)S(1)} custom-call(s32[5]{0:T(128)S(1)} %stack.19.info_ref, bf16[2,256,2560]{2,1,0:T(8,128)(2,1)S(1)} %collective-permute-done.2.refs_0_, bf16[2,2560,384]{2,1,0:T(8,128)(2,1)S(1)} %get-tuple-element.39.refs_2_.refs_1_, bf16[1,2560,384]{2,1,0:T(8,128)(2,1)S(1)} %get-tuple-element.42.refs_2_), custom_call_target="tpu_custom_call" | custom-call | flops 754974720 | bytes 7208960 | tf_op jit(solution)/shard_map/project/pallas_call | solution.py:46
  20.4 0.0 collective-permute-done.6.refs_3_
  20.4 0.0 collective-permute-done.5.refs_1_
  20.4 0.7 join.2.refs_4_
  21.0 0.0 collective-permute-done.4.refs_3_
  21.1 0.0 collective-permute-done.3.refs_1_
  21.1 1.7 %join.3 = bf16[8,704,128]{2,1,0:T(8,128)(2,1)} custom-call(s32[5]{0:T(128)S(1)} %stack.19.info_ref, f32[3,128,384]{2,1,0:T(8,128)S(1)} %get-tuple-element.40.refs_0_, f32[3,128,384]{2,1,0:T(8,128)S(1)} %collective-permute-done.3.refs_1_, f32[3,128,384]{2,1,0:T(8,128)S(1)} %project.8.refs_2_, f32[3,128,384]{2,1,0:T(8,128)S(1)} %collective-permute-done.4.refs_3_, ...), custom_call_target="tpu_custom_call" | custom-call | flops 294912 | bytes 2949120 | tf_op jit(solution)/shard_map/join/pallas_call | solution.py:46
  22.8 6.1 %all-to-all-start = ((bf16[8,704,128]{2,1,0:T(8,128)(2,1)}), bf16[8,704,128]{2,1,0:T(8,128)(2,1)S(1)}, u32[]{:S(2)}, u32[]{:S(2)}) async-start(bf16[8,704,128]{2,1,0:T(8,128)(2,1)} %join.3), calls=%async_computation | async-start | bytes 2883584 | tf_op jit(solution)/shard_map/all_to_all | solution.py:29
  28.8 0.3 collective-permute-start
  29.1 0.2 collective-permute-start.1
  29.3 19.3 %all-to-all-done.refs_2_.refs_3_ = bf16[8,704,128]{2,1,0:T(8,128)(2,1)S(1)} async-done(((bf16[8,704,128]{2,1,0:T(8,128)(2,1)}), bf16[8,704,128]{2,1,0:T(8,128)(2,1)S(1)}, u32[]{:S(2)}, u32[]{:S(2)}) %all-to-all-start) | async-done | bytes 1441824 | tf_op jit(solution)/shard_map/all_to_all | solution.py:29
  48.6 1.1 %collective-permute-start.7 = (bf16[8,704,128]{2,1,0:T(8,128)(2,1)S(1)}, bf16[8,704,128]{2,1,0:T(8,128)(2,1)S(1)}, u32[]{:S(2)}, u32[]{:S(2)}) collective-permute-start(bf16[8,704,128]{2,1,0:T(8,128)(2,1)S(1)} %all-to-all-done.refs_2_.refs_3_), channel_id=1, source_target_pairs={{0,64},{64,0},{1,65},{65,1},{2,66},{66,2},{3,67},{67,3},{4,68},{68... | collective-permute-start | bytes 4325384 | tf_op jit(solution)/shard_map/ppermute | solution.py:25
  49.7 2.8 %attend.2 = (bf16[384,2560]{1,0:T(8,128)(2,1)S(1)}, bf16[384,2560]{1,0:T(8,128)(2,1)S(1)}, f32[1536,128]{1,0:T(8,128)S(1)}, f32[1536,128]{1,0:T(8,128)S(1)}, f32[1536,128]{1,0:T(8,128)S(1)}) custom-call(s32[5]{0:T(128)S(1)} %stack.19.info_ref, bf16[384,2560]{1,0:T(8,128)(2,1)} %refs_0_.1, bf16[384,2560]{1,0:T(8,128)(2,1)} %refs_1_.1, ...), custom_call_target="tpu_custom_call" | custom-call | flops 805306368 | bytes 1310720 | tf_op jit(solution)/shard_map/attend/pallas_call | solution.py:46
  52.5 0.0 collective-permute-done.refs_0_
  52.6 0.0 collective-permute-done.7.refs_3_
  52.6 3.3 %attend.3 = (bf16[384,2560]{1,0:T(8,128)(2,1)S(1)}, bf16[384,2560]{1,0:T(8,128)(2,1)S(1)}, bf16[8,192,128]{2,1,0:T(8,128)(2,1)S(1)}, f32[8,128]{1,0:T(8,128)S(1)}) custom-call(s32[5]{0:T(128)S(1)} %stack.19.info_ref, bf16[384,2560]{1,0:T(8,128)(2,1)S(1)} %collective-permute-done.refs_0_, bf16[384,2560]{1,0:T(8,128)(2,1)} %collective-permute-done.1.refs_1_, ...), custom_call_target="tpu_custom_call" | custom-call | flops 805306368 | bytes 1310720 | tf_op jit(solution)/shard_map/attend/pallas_call | solution.py:46
  55.9 10.7 %all_to_all.10.attn_ref = bf16[8,192,128]{2,1,0:T(8,128)(2,1)S(1)} all-to-all(bf16[8,192,128]{2,1,0:T(8,128)(2,1)S(1)} %get-tuple-element.52), channel_id=1, replica_groups=mesh['dp'=2,'ctx'=8,'tp'=8] {'ctx'}, dimensions={0} | all-to-all | bytes 786432 | tf_op jit(solution)/shard_map/all_to_all | solution.py:29
  66.6 4.1 %expand.1 = (bf16[4,128,640]{2,1,0:T(8,128)(2,1)S(1)}, bf16[2,128,640]{2,1,0:T(8,128)(2,1)S(1)}, bf16[2,128,640]{2,1,0:T(8,128)(2,1)S(1)}, bf16[2,128,640]{2,1,0...) custom-call(s32[5]{0:T(128)S(1)} %stack.19.info_ref, ...), custom_call_target="tpu_custom_call" | custom-call | flops 2013265920 | bytes 7864320 | tf_op jit(solution)/shard_map/expand/pallas_call | solution.py:46
  70.7 2.5 %collective-permute-start.8 = (bf16[4,128,640]{2,1,0:T(8,128)(2,1)S(1)}, bf16[4,128,640]{2,1,0:T(8,128)(2,1)S(1)}, u32[]{:S(2)}, u32[]{:S(2)}) collective-permute-start(bf16[4,128,640]{2,1,0:T(8,128)(2,1)S(1)} %get-tuple-element.59), channel_id=1, source_target_pairs={{0,4},{1,5},{2,6},{3,7},{4,0},{5,1},{6,2},{7,3},{64,68},{65,69},{6... | collective-permute-start | bytes 1966088 | tf_op jit(solution)/shard_map/ppermute | solution.py:21
  73.2 2.9 %collective-permute-start.10 = (bf16[2,128,640]{2,1,0:T(8,128)(2,1)S(1)}, bf16[2,128,640]{2,1,0:T(8,128)(2,1)S(1)}, u32[]{:S(2)}, u32[]{:S(2)}) collective-permute-start(bf16[2,128,640]{2,1,0:T(8,128)(2,1)S(1)} %get-tuple-element.61), channel_id=1, source_target_pairs={{0,2},{1,3},{2,0},{3,1},{4,6},{5,7},{6,4},{7,5},{64,66},{65,67},{6... | collective-permute-start | bytes 983048 | tf_op jit(solution)/shard_map/ppermute | solution.py:21
  76.1 0.8 collective-permute-start.11
  76.9 0.7 collective-permute-start.9
  77.6 4.6 %collective-permute-done.10.refs_1_ = bf16[2,128,640]{2,1,0:T(8,128)(2,1)S(1)} collective-permute-done((bf16[2,128,640]{2,1,0:T(8,128)(2,1)S(1)}, bf16[2,128,640]{2,1,0:T(8,128)(2,1)S(1)}, u32[]{:S(2)}, u32[]{:S(2)}) %collective-permute-start.10) | collective-permute-done | bytes 327712 | tf_op jit(solution)/shard_map/ppermute | solution.py:21
  82.2 8.6 %collective-permute-done.11.refs_2_ = bf16[2,128,640]{2,1,0:T(8,128)(2,1)S(1)} collective-permute-done((bf16[2,128,640]{2,1,0:T(8,128)(2,1)S(1)}, bf16[2,128,640]{2,1,0:T(8,128)(2,1)S(1)}, u32[]{:S(2)}, u32[]{:S(2)}) %collective-permute-start.11) | collective-permute-done | bytes 327712 | tf_op jit(solution)/shard_map/ppermute | solution.py:21
  90.7 0.8 turn.1
  91.5 1.6 %collective-permute-start.13 = (f32[128,640]{1,0:T(8,128)S(1)}, f32[128,640]{1,0:T(8,128)S(1)}, u32[]{:S(2)}, u32[]{:S(2)}) collective-permute-start(f32[128,640]{1,0:T(8,128)S(1)} %get-tuple-element.65), channel_id=1, source_target_pairs={{0,64},{64,0},{1,65},{65,1},{2,66},{66,2},{3,67},{67,3},{4,68},{68... | collective-permute-start | bytes 983048 | tf_op jit(solution)/shard_map/ppermute | solution.py:25
  93.1 0.5 collective-permute-start.12
  93.7 1.3 %collective-permute-start.14 = (bf16[128,640]{1,0:T(8,128)(2,1)S(1)}, bf16[128,640]{1,0:T(8,128)(2,1)S(1)}, u32[]{:S(2)}, u32[]{:S(2)}) collective-permute-start(bf16[128,640]{1,0:T(8,128)(2,1)S(1)} %get-tuple-element.66), channel_id=1, source_target_pairs={{0,65},{1,66},{2,67},{3,64},{4,69},{5,70},{6,71},{7,68},{64,1},{65... | collective-permute-start | bytes 491528 | tf_op jit(solution)/shard_map/ppermute | solution.py:21
  95.0 2.5 %collective-permute-start.15 = (bf16[128,640]{1,0:T(8,128)(2,1)S(1)}, bf16[128,640]{1,0:T(8,128)(2,1)S(1)}, u32[]{:S(2)}, u32[]{:S(2)}) collective-permute-start(bf16[128,640]{1,0:T(8,128)(2,1)S(1)} %get-tuple-element.67), channel_id=1, source_target_pairs={{0,66},{1,67},{2,64},{3,65},{4,70},{5,71},{6,68},{7,69},{64,2},{65... | collective-permute-start | bytes 491528 | tf_op jit(solution)/shard_map/ppermute | solution.py:21
  97.5 1.3 %collective-permute-start.16 = (bf16[128,640]{1,0:T(8,128)(2,1)S(1)}, bf16[128,640]{1,0:T(8,128)(2,1)S(1)}, u32[]{:S(2)}, u32[]{:S(2)}) collective-permute-start(bf16[128,640]{1,0:T(8,128)(2,1)S(1)} %get-tuple-element.68), channel_id=1, source_target_pairs={{0,67},{1,64},{2,65},{3,66},{4,71},{5,68},{6,69},{7,70},{64,3},{65... | collective-permute-start | bytes 491528 | tf_op jit(solution)/shard_map/ppermute | solution.py:21
  98.8 1.6 %collective-permute-done.12.x_ref = bf16[128,640]{1,0:T(8,128)(2,1)S(1)} collective-permute-done((bf16[128,640]{1,0:T(8,128)(2,1)S(1)}, bf16[128,640]{1,0:T(8,128)(2,1)S(1)}, u32[]{:S(2)}, u32[]{:S(2)}) %collective-permute-start.12) | collective-permute-done | bytes 163872 | tf_op jit(solution)/shard_map/ppermute | solution.py:21
  100.4 0.7 collective-permute-done.14.refs_0_
  101.1 4.4 %collective-permute-done.15.refs_1_ = bf16[128,640]{1,0:T(8,128)(2,1)S(1)} collective-permute-done((bf16[128,640]{1,0:T(8,128)(2,1)S(1)}, bf16[128,640]{1,0:T(8,128)(2,1)S(1)}, u32[]{:S(2)}, u32[]{:S(2)}) %collective-permute-start.15) | collective-permute-done | bytes 163872 | tf_op jit(solution)/shard_map/ppermute | solution.py:21
  105.4 0.0 collective-permute-done.16.refs_2_
  105.4 0.0 collective-permute-done.13.other_ref
  105.4 1.5 %collect.1 = bf16[256,640]{1,0:T(8,128)(2,1)} custom-call(s32[5]{0:T(128)S(1)} %stack.19.info_ref, f32[8,128]{1,0:T(8,128)S(1)} %get-tuple-element.51.level_ref, f32[128,640]{1,0:T(8,128)S(1)} %get-tuple-element.63.own_ref, bf16[128,640]{1,0:T(8,128)(2,1)S(1)} %collective-permute-done.12.x_ref, f32[128,640]{1,0:T(8,128)S(1)} %collective-permute-done.13.other_ref, ...), custom_call_target="tpu_custom_call" | custom-call | tf_op jit(solution)/shard_map/collect/pallas_call | solution.py:487
  (3 shorter events, 0.0 us)
Async XLA Ops:
  5.9 8.2 %collective-permute-start.2 = (bf16[2,256,2560]{2,1,0:T(8,128)(2,1)S(1)}, bf16[2,256,2560]{2,1,0:T(8,128)(2,1)S(1)}, u32[]{:S(2)}, u32[]{:S(2)}) collective-permute-start(bf16[2,256,2560]{2,1,0:T(8,128)(2,1)S(1)} %get-tuple-element.41), channel_id=1, source_target_pairs={{0,64},{64,0},{1,65},{65,1},{2,66},{66,2},{3,67},{67,3},{4,68},{68... | collective-permute-start | bytes 7864328 | tf_op jit(solution)/shard_map/ppermute | solution.py:25
  10.1 10.3 %collective-permute-start.6 = (f32[3,128,384]{2,1,0:T(8,128)S(1)}, f32[3,128,384]{2,1,0:T(8,128)S(1)}, u32[]{:S(2)}, u32[]{:S(2)}) collective-permute-start(f32[3,128,384]{2,1,0:T(8,128)S(1)} %get-tuple-element.47), channel_id=1, source_target_pairs={{0,64},{64,0},{1,65},{65,1},{2,66},{66,2},{3,67},{67,3},{4,68},{68... | collective-permute-start | bytes 1769480 | tf_op jit(solution)/shard_map/ppermute | solution.py:25
  13.5 7.6 %collective-permute-start.4 = (f32[3,128,384]{2,1,0:T(8,128)S(1)}, f32[3,128,384]{2,1,0:T(8,128)S(1)}, u32[]{:S(2)}, u32[]{:S(2)}) collective-permute-start(f32[3,128,384]{2,1,0:T(8,128)S(1)} %get-tuple-element.43), channel_id=1, source_target_pairs={{0,64},{64,0},{1,65},{65,1},{2,66},{66,2},{3,67},{67,3},{4,68},{68... | collective-permute-start | bytes 1769480 | tf_op jit(solution)/shard_map/ppermute | solution.py:25
  16.5 3.9 %collective-permute-start.5 = (f32[3,128,384]{2,1,0:T(8,128)S(1)}, f32[3,128,384]{2,1,0:T(8,128)S(1)}, u32[]{:S(2)}, u32[]{:S(2)}) collective-permute-start(f32[3,128,384]{2,1,0:T(8,128)S(1)} %get-tuple-element.45), channel_id=1, source_target_pairs={{0,64},{64,0},{1,65},{65,1},{2,66},{66,2},{3,67},{67,3},{4,68},{68... | collective-permute-start | bytes 1769480 | tf_op jit(solution)/shard_map/ppermute | solution.py:25
  18.2 2.9 %collective-permute-start.3 = (f32[3,128,384]{2,1,0:T(8,128)S(1)}, f32[3,128,384]{2,1,0:T(8,128)S(1)}, u32[]{:S(2)}, u32[]{:S(2)}) collective-permute-start(f32[3,128,384]{2,1,0:T(8,128)S(1)} %project.7), channel_id=1, source_target_pairs={{0,64},{64,0},{1,65},{65,1},{2,66},{66,2},{3,67},{67,3},{4,68},{68... | collective-permute-start | bytes 1769480 | tf_op jit(solution)/shard_map/ppermute | solution.py:25
  22.8 25.8 %all-to-all-start = ((bf16[8,704,128]{2,1,0:T(8,128)(2,1)}), bf16[8,704,128]{2,1,0:T(8,128)(2,1)S(1)}, u32[]{:S(2)}, u32[]{:S(2)}) async-start(bf16[8,704,128]{2,1,0:T(8,128)(2,1)} %join.3), calls=%async_computation | async-start | bytes 2883584 | tf_op jit(solution)/shard_map/all_to_all | solution.py:29
  28.8 23.7 %collective-permute-start = (bf16[384,2560]{1,0:T(8,128)(2,1)}, bf16[384,2560]{1,0:T(8,128)(2,1)S(1)}, u32[]{:S(2)}, u32[]{:S(2)}) collective-permute-start(bf16[384,2560]{1,0:T(8,128)(2,1)} %refs_0_.1), channel_id=1, source_target_pairs={{0,64},{64,0},{1,65},{65,1},{2,66},{66,2},{3,67},{67,3},{4,68},{68... | collective-permute-start | bytes 5898248 | tf_op jit(solution)/shard_map/ppermute | solution.py:25
  29.1 23.4 %collective-permute-start.1 = (bf16[384,2560]{1,0:T(8,128)(2,1)}, bf16[384,2560]{1,0:T(8,128)(2,1)}, u32[]{:S(2)}, u32[]{:S(2)}) collective-permute-start(bf16[384,2560]{1,0:T(8,128)(2,1)} %refs_1_.1), channel_id=1, source_target_pairs={{0,64},{64,0},{1,65},{65,1},{2,66},{66,2},{3,67},{67,3},{4,68},{68... | collective-permute-start | bytes 5898248 | tf_op jit(solution)/shard_map/ppermute | solution.py:25
  48.6 4.0 %collective-permute-start.7 = (bf16[8,704,128]{2,1,0:T(8,128)(2,1)S(1)}, bf16[8,704,128]{2,1,0:T(8,128)(2,1)S(1)}, u32[]{:S(2)}, u32[]{:S(2)}) collective-permute-start(bf16[8,704,128]{2,1,0:T(8,128)(2,1)S(1)} %all-to-all-done.refs_2_.refs_3_), channel_id=1, source_target_pairs={{0,64},{64,0},{1,65},{65,1},{2,66},{66,2},{3,67},{67,3},{4,68},{68... | collective-permute-start | bytes 4325384 | tf_op jit(solution)/shard_map/ppermute | solution.py:25
  70.7 20.0 %collective-permute-start.8 = (bf16[4,128,640]{2,1,0:T(8,128)(2,1)S(1)}, bf16[4,128,640]{2,1,0:T(8,128)(2,1)S(1)}, u32[]{:S(2)}, u32[]{:S(2)}) collective-permute-start(bf16[4,128,640]{2,1,0:T(8,128)(2,1)S(1)} %get-tuple-element.59), channel_id=1, source_target_pairs={{0,4},{1,5},{2,6},{3,7},{4,0},{5,1},{6,2},{7,3},{64,68},{65,69},{6... | collective-permute-start | bytes 1966088 | tf_op jit(solution)/shard_map/ppermute | solution.py:21
  73.2 8.9 %collective-permute-start.10 = (bf16[2,128,640]{2,1,0:T(8,128)(2,1)S(1)}, bf16[2,128,640]{2,1,0:T(8,128)(2,1)S(1)}, u32[]{:S(2)}, u32[]{:S(2)}) collective-permute-start(bf16[2,128,640]{2,1,0:T(8,128)(2,1)S(1)} %get-tuple-element.61), channel_id=1, source_target_pairs={{0,2},{1,3},{2,0},{3,1},{4,6},{5,7},{6,4},{7,5},{64,66},{65,67},{6... | collective-permute-start | bytes 983048 | tf_op jit(solution)/shard_map/ppermute | solution.py:21
  76.1 14.6 %collective-permute-start.11 = (bf16[2,128,640]{2,1,0:T(8,128)(2,1)S(1)}, bf16[2,128,640]{2,1,0:T(8,128)(2,1)S(1)}, u32[]{:S(2)}, u32[]{:S(2)}) collective-permute-start(bf16[2,128,640]{2,1,0:T(8,128)(2,1)S(1)} %get-tuple-element.62), channel_id=1, source_target_pairs={{0,3},{1,0},{2,1},{3,2},{4,7},{5,4},{6,5},{7,6},{64,67},{65,64},{6... | collective-permute-start | bytes 983048 | tf_op jit(solution)/shard_map/ppermute | solution.py:21
  76.9 13.8 %collective-permute-start.9 = (bf16[2,128,640]{2,1,0:T(8,128)(2,1)S(1)}, bf16[2,128,640]{2,1,0:T(8,128)(2,1)S(1)}, u32[]{:S(2)}, u32[]{:S(2)}) collective-permute-start(bf16[2,128,640]{2,1,0:T(8,128)(2,1)S(1)} %get-tuple-element.60), channel_id=1, source_target_pairs={{0,1},{1,2},{2,3},{3,0},{4,5},{5,6},{6,7},{7,4},{64,65},{65,66},{6... | collective-permute-start | bytes 983048 | tf_op jit(solution)/shard_map/ppermute | solution.py:21
  91.5 13.9 %collective-permute-start.13 = (f32[128,640]{1,0:T(8,128)S(1)}, f32[128,640]{1,0:T(8,128)S(1)}, u32[]{:S(2)}, u32[]{:S(2)}) collective-permute-start(f32[128,640]{1,0:T(8,128)S(1)} %get-tuple-element.65), channel_id=1, source_target_pairs={{0,64},{64,0},{1,65},{65,1},{2,66},{66,2},{3,67},{67,3},{4,68},{68... | collective-permute-start | bytes 983048 | tf_op jit(solution)/shard_map/ppermute | solution.py:25
  93.1 7.3 %collective-permute-start.12 = (bf16[128,640]{1,0:T(8,128)(2,1)S(1)}, bf16[128,640]{1,0:T(8,128)(2,1)S(1)}, u32[]{:S(2)}, u32[]{:S(2)}) collective-permute-start(bf16[128,640]{1,0:T(8,128)(2,1)S(1)} %get-tuple-element.64), channel_id=1, source_target_pairs={{0,4},{1,5},{2,6},{3,7},{4,0},{5,1},{6,2},{7,3},{64,68},{65,69},{6... | collective-permute-start | bytes 491528 | tf_op jit(solution)/shard_map/ppermute | solution.py:21
  93.7 7.4 %collective-permute-start.14 = (bf16[128,640]{1,0:T(8,128)(2,1)S(1)}, bf16[128,640]{1,0:T(8,128)(2,1)S(1)}, u32[]{:S(2)}, u32[]{:S(2)}) collective-permute-start(bf16[128,640]{1,0:T(8,128)(2,1)S(1)} %get-tuple-element.66), channel_id=1, source_target_pairs={{0,65},{1,66},{2,67},{3,64},{4,69},{5,70},{6,71},{7,68},{64,1},{65... | collective-permute-start | bytes 491528 | tf_op jit(solution)/shard_map/ppermute | solution.py:21
  95.0 10.5 %collective-permute-start.15 = (bf16[128,640]{1,0:T(8,128)(2,1)S(1)}, bf16[128,640]{1,0:T(8,128)(2,1)S(1)}, u32[]{:S(2)}, u32[]{:S(2)}) collective-permute-start(bf16[128,640]{1,0:T(8,128)(2,1)S(1)} %get-tuple-element.67), channel_id=1, source_target_pairs={{0,66},{1,67},{2,64},{3,65},{4,70},{5,71},{6,68},{7,69},{64,2},{65... | collective-permute-start | bytes 491528 | tf_op jit(solution)/shard_map/ppermute | solution.py:21
  97.5 7.9 %collective-permute-start.16 = (bf16[128,640]{1,0:T(8,128)(2,1)S(1)}, bf16[128,640]{1,0:T(8,128)(2,1)S(1)}, u32[]{:S(2)}, u32[]{:S(2)}) collective-permute-start(bf16[128,640]{1,0:T(8,128)(2,1)S(1)} %get-tuple-element.68), channel_id=1, source_target_pairs={{0,67},{1,64},{2,65},{3,66},{4,71},{5,68},{6,69},{7,70},{64,3},{65... | collective-permute-start | bytes 491528 | tf_op jit(solution)/shard_map/ppermute | solution.py:21

commit v3 on v2

--- a/solution.py
+++ b/solution.py
@@ -378,19 +378,20 @@
     )
 
 
-def expand(info, attn, mine, other):
+def expand(info, attn, mine, other, leaving):
     _, size, _ = attn.shape
     half = size // 3
     rows, panel = 2 * half, 3 * HD
-    columns = mine[0].shape[1]
-    part = columns // Y
+    part = mine[0].shape[1] // Y
+    shifts = range(1, Y) if leaving else (0,)
 
     def body(info_ref, attn_ref, *refs):
-        weights, (to_x, *to_y, own_y, own_x, left) = refs[:4], refs[4:]
+        weights, (by_x, *by_y, left) = refs[:4], refs[4:]
+        core = info_ref[AT_CORE]
         for unit in range(UNITS):
             model, clip, j = unit // 4, unit // 2 % 2, unit % 2
             lane = model * panel
-            line = lax.rem(clip + info_ref[AT_CORE], 2) * rows
+            line = lax.rem(clip + core, 2) * rows
             left[
                 pl.ds(pl.multiple_of(line, rows), rows),
                 lane + 2 * j * HD : lane + (2 * j + 1) * HD,
@@ -399,42 +400,43 @@
             left[pl.ds(pl.multiple_of(line, half), half), lane + HD : lane + 2 * HD] = attn_ref[
                 unit, rows:
             ]
-        for i in range(0, 8, 2):
-            place = slice(i % 4 * part, (i % 4 + 2) * part)
-            right = jnp.concatenate([w[:, place] for w in weights[i // 4 * 2 : i // 4 * 2 + 2]])
-            value = jnp.dot(left[...], right, preferred_element_type=F32)
-            xh = info_ref[AT_CORE] if i < 4 else 1 - info_ref[AT_CORE]
-            here = xh == info_ref[AT_XH]
-            for n in range(2):
-                y = i % 4 + n
-                shift = lax.rem(y - info_ref[AT_Y] + Y, Y)
-                first = value[:rows, n * part : (n + 1) * part]
-                second = value[rows:, n * part : (n + 1) * part]
-                for f, target in enumerate((own_y, *to_y)):
-
-                    @pl.when(shift == f)
-                    def _():
-                        target[xh] = first.astype(target.dtype)
-
-                @pl.when(here)
-                def _():
-                    own_x[y] = second
-
-                @pl.when(jnp.logical_not(here))
-                def _():
-                    to_x[y] = second.astype(BF16)
-
-    by_x, by_y = (Y, rows, part), (XH, rows, part)
+
+        def over_x(pair):
+            for y in range(0, Y, 2):
+                columns = slice(y * part, (y + 2) * part)
+                right = jnp.concatenate([w[:, columns] for w in pair])
+                value = jnp.dot(left[rows:], right, preferred_element_type=F32)
+                for n in range(2):
+                    by_x[y + n] = value[:, n * part : (n + 1) * part].astype(by_x.dtype)
+
+        near = (core == info_ref[AT_XH]) != leaving
+        pl.when(near)(lambda: over_x(weights[:2]))
+        pl.when(jnp.logical_not(near))(lambda: over_x(weights[2:]))
+        for shift, out in zip(shifts, by_y):
+            place = lax.rem(info_ref[AT_Y] + shift, Y) * part
+            columns = pl.ds(pl.multiple_of(place, HD), part)
+            right = jnp.concatenate(
+                [
+                    jnp.concatenate([w[:, columns] for w in pair])
+                    for pair in (weights[:2], weights[2:])
+                ],
+                axis=1,
+            )
+            value = jnp.dot(left[:rows], right, preferred_element_type=F32).astype(out.dtype)
+            out[core] = value[:, :part]
+            out[1 - core] = value[:, part:]
+
+    kind = BF16 if leaving else F32
     return kernel(
         body,
         "expand",
         info,
         (),
         (attn, *mine, *other),
-        ((by_x, BF16), *[(by_y, BF16)] * (Y - 1), (by_y, F32), (by_x, F32)),
+        (((Y, rows, part), kind), *[((XH, rows, part), kind)] * len(shifts)),
         12,
-        16 * rows * panel * columns,
-        8 * panel * columns,
+        8 * rows * panel * part * Y,
+        8 * panel * part * Y,
         scratch=(pltpu.VMEM((2 * rows, 2 * panel), BF16),),
     )
 
@@ -528,9 +530,11 @@
     block = exchange(blocks, "ctx")
     *mine, peak, total, summed = attend(info, block, block, [in_hbm(out) for out in outs])
     *other, attn, level = attend(info, block, swapped(block), other, (peak, total, summed))
-    to_x, *to_y, own_y, own_x = expand(info, exchange(attn, "ctx"), mine, other)
+    attn = exchange(attn, "ctx")
+    to_x, *to_y = expand(info, attn, mine, other, True)
     from_x = over_tp(to_x, 1, 0)
     from_y = [over_tp(value, 0, f) for f, value in enumerate(to_y, 1)]
+    own_x, own_y = expand(info, attn, mine, other, False)
     own, other, to_x, *to_y = turn(info, own_y, own_x, from_x, from_y)
     from_x = over_tp(to_x, 1, 0)
     from_y = [over_tp(value, 0, f, 1) for f, value in enumerate(to_y, 1)]

time: 107 us -> 105 us (0.981)
  waiting for transfers between devices: 39.1 us -> 37.3 us
    ppermute x8, waiting for transfers between devices: 19.8 us -> 18 us  [over_tp(): return lax.ppermute(value, ('dp', 'tp'), pairs)]
    pallas_call x12 -> x13, Pallas kernels: 30.1 us -> 30 us  [kernel(): pl.pallas_call(body, in_specs=[SCALAR] + [ANYWHERE] * len(far) + [NEAR] *...]
  transfers between devices with their start and end apart: 18 -> 18, of which waited for: 6 -> 6; matrix products, arithmetic and copies ran while one was open for 0% -> 0% of each run, Pallas kernels for 14% -> 16%
where the time goes in v3:
time: 105 us
  waiting for transfers between devices  37.3 us (36%)
  Pallas kernels  31.5 us (30%)
  starting transfers between devices  24.7 us (24%)
  blocking collectives  10.7 us (10%)
    pallas_call x13, Pallas kernels, kernel(): pl.pallas_call(body, in_specs=[SCALAR] + [ANYWHERE] * len(far) + [NEAR] *...  30 us
    all_to_all x1, waiting for transfers between devices, exchange(): return lax.all_to_all(value, axes, 0, 0, tiled=True)  19.3 us
    ppermute x8, waiting for transfers between devices, over_tp(): return lax.ppermute(value, ('dp', 'tp'), pairs)  18 us
    ppermute x8, starting transfers between devices, over_tp(): return lax.ppermute(value, ('dp', 'tp'), pairs)  12.6 us
    all_to_all x1, blocking collectives, exchange(): return lax.all_to_all(value, axes, 0, 0, tiled=True)  10.7 us
    ppermute x9, starting transfers between devices, swapped(): return lax.ppermute(value, 'dp', [(0, 1), (1, 0)])  6.08 us
    all_to_all x1, starting transfers between devices, exchange(): return lax.all_to_all(value, axes, 0, 0, tiled=True)  6.06 us
  transfers between devices with their start and end apart: 18, of which 6 were waited for; matrix products, arithmetic and copies ran while one was open for 0% of the time, Pallas kernels for 16%

profile of v3, /device:TPU:1, one launch (start us, length us, event | category | flops | bytes accessed | tf_op | source)
XLA Modules:
  0.0 105.1 jit_solution(4897221820302584856)
XLA Ops:
  0.7 0.1 stack.19.info_ref
  0.7 5.1 %norm.1 = (bf16[2,256,2560]{2,1,0:T(8,128)(2,1)S(1)}, bf16[2,256,2560]{2,1,0:T(8,128)(2,1)S(1)}, bf16[3,2560,384]{2,1,0:T(8,128)(2,1)S(1)}) custom-call(s32[5]{0:T(128)S(1)} %stack.19.info_ref, bf16[256,5120]{1,0:T(8,128)(2,1)} %bitcast.14, bf16[256,5120]{1,0:T(8,128)(2,1)} %bitcast.15, f32[40,128]{1,0:T(8,128)} %bitcast.16, f32[40,128]{1,0:T(8,128)} %bitcast.17, ...), custom_call_target="tpu_custom_call" | custom-call | flops 13107200 | bytes 10485760 | tf_op jit(solution)/shard_map/norm/pallas_call | solution.py:46
  5.9 1.5 %collective-permute-start.2 = (bf16[2,256,2560]{2,1,0:T(8,128)(2,1)S(1)}, bf16[2,256,2560]{2,1,0:T(8,128)(2,1)S(1)}, u32[]{:S(2)}, u32[]{:S(2)}) collective-permute-start(bf16[2,256,2560]{2,1,0:T(8,128)(2,1)S(1)} %get-tuple-element.41), channel_id=1, source_target_pairs={{0,64},{64,0},{1,65},{65,1},{2,66},{66,2},{3,67},{67,3},{4,68},{68... | collective-permute-start | bytes 7864328 | tf_op jit(solution)/shard_map/ppermute | solution.py:25
  7.4 2.7 %project.5 = (f32[3,128,384]{2,1,0:T(8,128)S(1)}, f32[3,128,384]{2,1,0:T(8,128)S(1)}, bf16[2,2560,384]{2,1,0:T(8,128)(2,1)S(1)}) custom-call(s32[5]{0:T(128)S(1)} %stack.19.info_ref, bf16[3,2560,384]{2,1,0:T(8,128)(2,1)} %bitcast.11, bf16[2,256,2560]{2,1,0:T(8,128)(2,1)S(1)} %get-tuple-element.37.refs_1_, ...), custom_call_target="tpu_custom_call" | custom-call | flops 1509949440 | bytes 7208960 | tf_op jit(solution)/shard_map/project/pallas_call | solution.py:46
  10.1 0.1 collective-permute-start.6
  10.2 3.3 %project.6 = (f32[3,128,384]{2,1,0:T(8,128)S(1)}, f32[3,128,384]{2,1,0:T(8,128)S(1)}, bf16[1,2560,384]{2,1,0:T(8,128)(2,1)S(1)}) custom-call(s32[5]{0:T(128)S(1)} %stack.19.info_ref, bf16[3,2560,384]{2,1,0:T(8,128)(2,1)} %bitcast.12, bf16[2,256,2560]{2,1,0:T(8,128)(2,1)S(1)} %get-tuple-element.37.refs_1_, ...), custom_call_target="tpu_custom_call" | custom-call | flops 1509949440 | bytes 7208960 | tf_op jit(solution)/shard_map/project/pallas_call | solution.py:46
  13.5 0.6 collective-permute-start.4
  14.1 0.0 collective-permute-done.2.refs_0_
  14.1 2.4 %project.9 = (f32[3,128,384]{2,1,0:T(8,128)S(1)}, f32[3,128,384]{2,1,0:T(8,128)S(1)}) custom-call(s32[5]{0:T(128)S(1)} %stack.19.info_ref, bf16[2,256,2560]{2,1,0:T(8,128)(2,1)S(1)} %collective-permute-done.2.refs_0_, bf16[3,2560,384]{2,1,0:T(8,128)(2,1)S(1)} %get-tuple-element.38.refs_2_.refs_1_), custom_call_target="tpu_custom_call" | custom-call | flops 1509949440 | bytes 7208960 | tf_op jit(solution)/shard_map/project/pallas_call | solution.py:46
  16.5 0.1 collective-permute-start.5
  16.6 1.6 %project.7 = f32[3,128,384]{2,1,0:T(8,128)S(1)} custom-call(s32[5]{0:T(128)S(1)} %stack.19.info_ref, bf16[2,256,2560]{2,1,0:T(8,128)(2,1)S(1)} %collective-permute-done.2.refs_0_, bf16[2,2560,384]{2,1,0:T(8,128)(2,1)S(1)} %get-tuple-element.39.refs_2_.refs_1_, bf16[1,2560,384]{2,1,0:T(8,128)(2,1)S(1)} %get-tuple-element.42.refs_2_), custom_call_target="tpu_custom_call" | custom-call | flops 754974720 | bytes 7208960 | tf_op jit(solution)/shard_map/project/pallas_call | solution.py:46
  18.2 0.6 collective-permute-start.3
  18.8 1.6 %project.8.refs_2_ = f32[3,128,384]{2,1,0:T(8,128)S(1)} custom-call(s32[5]{0:T(128)S(1)} %stack.19.info_ref, bf16[2,256,2560]{2,1,0:T(8,128)(2,1)S(1)} %collective-permute-done.2.refs_0_, bf16[2,2560,384]{2,1,0:T(8,128)(2,1)S(1)} %get-tuple-element.39.refs_2_.refs_1_, bf16[1,2560,384]{2,1,0:T(8,128)(2,1)S(1)} %get-tuple-element.42.refs_2_), custom_call_target="tpu_custom_call" | custom-call | flops 754974720 | bytes 7208960 | tf_op jit(solution)/shard_map/project/pallas_call | solution.py:46
  20.4 0.0 collective-permute-done.6.refs_3_
  20.4 0.0 collective-permute-done.5.refs_1_
  20.4 0.7 join.2.refs_4_
  21.1 0.0 collective-permute-done.3.refs_1_
  21.1 1.7 %join.3 = bf16[8,704,128]{2,1,0:T(8,128)(2,1)} custom-call(s32[5]{0:T(128)S(1)} %stack.19.info_ref, f32[3,128,384]{2,1,0:T(8,128)S(1)} %get-tuple-element.40.refs_0_, f32[3,128,384]{2,1,0:T(8,128)S(1)} %collective-permute-done.3.refs_1_, f32[3,128,384]{2,1,0:T(8,128)S(1)} %project.8.refs_2_, f32[3,128,384]{2,1,0:T(8,128)S(1)} %collective-permute-done.4.refs_3_, ...), custom_call_target="tpu_custom_call" | custom-call | flops 294912 | bytes 2949120 | tf_op jit(solution)/shard_map/join/pallas_call | solution.py:46
  22.8 6.1 %all-to-all-start = ((bf16[8,704,128]{2,1,0:T(8,128)(2,1)}), bf16[8,704,128]{2,1,0:T(8,128)(2,1)S(1)}, u32[]{:S(2)}, u32[]{:S(2)}) async-start(bf16[8,704,128]{2,1,0:T(8,128)(2,1)} %join.3), calls=%async_computation | async-start | bytes 2883584 | tf_op jit(solution)/shard_map/all_to_all | solution.py:29
  28.8 0.3 collective-permute-start
  29.1 0.2 collective-permute-start.1
  29.4 19.3 %all-to-all-done.refs_2_.refs_3_ = bf16[8,704,128]{2,1,0:T(8,128)(2,1)S(1)} async-done(((bf16[8,704,128]{2,1,0:T(8,128)(2,1)}), bf16[8,704,128]{2,1,0:T(8,128)(2,1)S(1)}, u32[]{:S(2)}, u32[]{:S(2)}) %all-to-all-start) | async-done | bytes 1441824 | tf_op jit(solution)/shard_map/all_to_all | solution.py:29
  48.6 1.1 %collective-permute-start.7 = (bf16[8,704,128]{2,1,0:T(8,128)(2,1)S(1)}, bf16[8,704,128]{2,1,0:T(8,128)(2,1)S(1)}, u32[]{:S(2)}, u32[]{:S(2)}) collective-permute-start(bf16[8,704,128]{2,1,0:T(8,128)(2,1)S(1)} %all-to-all-done.refs_2_.refs_3_), channel_id=1, source_target_pairs={{0,64},{64,0},{1,65},{65,1},{2,66},{66,2},{3,67},{67,3},{4,68},{68... | collective-permute-start | bytes 4325384 | tf_op jit(solution)/shard_map/ppermute | solution.py:25
  49.8 2.8 %attend.2 = (bf16[384,2560]{1,0:T(8,128)(2,1)S(1)}, bf16[384,2560]{1,0:T(8,128)(2,1)S(1)}, f32[1536,128]{1,0:T(8,128)S(1)}, f32[1536,128]{1,0:T(8,128)S(1)}, f32[1536,128]{1,0:T(8,128)S(1)}) custom-call(s32[5]{0:T(128)S(1)} %stack.19.info_ref, bf16[384,2560]{1,0:T(8,128)(2,1)} %refs_0_.1, bf16[384,2560]{1,0:T(8,128)(2,1)} %refs_1_.1, ...), custom_call_target="tpu_custom_call" | custom-call | flops 805306368 | bytes 1310720 | tf_op jit(solution)/shard_map/attend/pallas_call | solution.py:46
  52.6 0.0 collective-permute-done.refs_0_
  52.6 0.0 collective-permute-done.7.refs_3_
  52.6 3.3 %attend.3 = (bf16[384,2560]{1,0:T(8,128)(2,1)S(1)}, bf16[384,2560]{1,0:T(8,128)(2,1)S(1)}, bf16[8,192,128]{2,1,0:T(8,128)(2,1)S(1)}, f32[8,128]{1,0:T(8,128)S(1)}) custom-call(s32[5]{0:T(128)S(1)} %stack.19.info_ref, bf16[384,2560]{1,0:T(8,128)(2,1)S(1)} %collective-permute-done.refs_0_, bf16[384,2560]{1,0:T(8,128)(2,1)} %collective-permute-done.1.refs_1_, ...), custom_call_target="tpu_custom_call" | custom-call | flops 805306368 | bytes 1310720 | tf_op jit(solution)/shard_map/attend/pallas_call | solution.py:46
  55.9 10.7 %all_to_all.10.attn_ref = bf16[8,192,128]{2,1,0:T(8,128)(2,1)S(1)} all-to-all(bf16[8,192,128]{2,1,0:T(8,128)(2,1)S(1)} %get-tuple-element.52), channel_id=1, replica_groups=mesh['dp'=2,'ctx'=8,'tp'=8] {'ctx'}, dimensions={0} | all-to-all | bytes 786432 | tf_op jit(solution)/shard_map/all_to_all | solution.py:29
  66.6 2.3 %expand.3 = (bf16[4,128,640]{2,1,0:T(8,128)(2,1)S(1)}, bf16[2,128,640]{2,1,0:T(8,128)(2,1)S(1)}, bf16[2,128,640]{2,1,0:T(8,128)(2,1)S(1)}, bf16[2,128,640]{2,1,0:T(8,128)(2,1)S(1)}) custom-call(s32[5]{0:T(128)S(1)} %stack.19.info_ref, bf16[8,192,128]{2,1,0:T(8,128)(2,1)S(1)} %all_to_all.10.attn_ref, bf16[384,2560]{1,0:T(8,128)(2,1)S(1)} %get-tuple-element.53.refs_0_, ...), custom_call_target="tpu_custom_call" | custom-call | flops 1006632960 | bytes 7864320 | tf_op jit(solution)/shard_map/expand/pallas_call | solution.py:46
  68.9 2.5 %collective-permute-start.8 = (bf16[4,128,640]{2,1,0:T(8,128)(2,1)S(1)}, bf16[4,128,640]{2,1,0:T(8,128)(2,1)S(1)}, u32[]{:S(2)}, u32[]{:S(2)}) collective-permute-start(bf16[4,128,640]{2,1,0:T(8,128)(2,1)S(1)} %get-tuple-element.59), channel_id=1, source_target_pairs={{0,4},{1,5},{2,6},{3,7},{4,0},{5,1},{6,2},{7,3},{64,68},{65,69},{6... | collective-permute-start | bytes 1966088 | tf_op jit(solution)/shard_map/ppermute | solution.py:21
  71.4 2.9 %collective-permute-start.10 = (bf16[2,128,640]{2,1,0:T(8,128)(2,1)S(1)}, bf16[2,128,640]{2,1,0:T(8,128)(2,1)S(1)}, u32[]{:S(2)}, u32[]{:S(2)}) collective-permute-start(bf16[2,128,640]{2,1,0:T(8,128)(2,1)S(1)} %get-tuple-element.61), channel_id=1, source_target_pairs={{0,2},{1,3},{2,0},{3,1},{4,6},{5,7},{6,4},{7,5},{64,66},{65,67},{6... | collective-permute-start | bytes 983048 | tf_op jit(solution)/shard_map/ppermute | solution.py:21
  74.3 0.8 collective-permute-start.11
  75.1 0.7 collective-permute-start.9
  75.8 1.7 %expand.2 = (f32[4,128,640]{2,1,0:T(8,128)S(1)}, f32[2,128,640]{2,1,0:T(8,128)S(1)}) custom-call(s32[5]{0:T(128)S(1)} %stack.19.info_ref, bf16[8,192,128]{2,1,0:T(8,128)(2,1)S(1)} %all_to_all.10.attn_ref, bf16[384,2560]{1,0:T(8,128)(2,1)S(1)} %get-tuple-element.53.refs_0_, bf16[384,2560]{1,0:T(8,128)(2,1)S(1)} %get-tuple-element.54.refs_1_, ...), custom_call_target="tpu_custom_call" | custom-call | flops 1006632960 | bytes 7864320 | tf_op jit(solution)/shard_map/expand/pallas_call | solution.py:46
  77.5 2.8 %collective-permute-done.10.refs_1_ = bf16[2,128,640]{2,1,0:T(8,128)(2,1)S(1)} collective-permute-done((bf16[2,128,640]{2,1,0:T(8,128)(2,1)S(1)}, bf16[2,128,640]{2,1,0:T(8,128)(2,1)S(1)}, u32[]{:S(2)}, u32[]{:S(2)}) %collective-permute-start.10) | collective-permute-done | bytes 327712 | tf_op jit(solution)/shard_map/ppermute | solution.py:21
  80.3 8.5 %collective-permute-done.11.refs_2_ = bf16[2,128,640]{2,1,0:T(8,128)(2,1)S(1)} collective-permute-done((bf16[2,128,640]{2,1,0:T(8,128)(2,1)S(1)}, bf16[2,128,640]{2,1,0:T(8,128)(2,1)S(1)}, u32[]{:S(2)}, u32[]{:S(2)}) %collective-permute-start.11) | collective-permute-done | bytes 327712 | tf_op jit(solution)/shard_map/ppermute | solution.py:21
  88.9 0.0 collective-permute-done.9.refs_0_
  88.9 0.0 collective-permute-done.8.from_x_ref
  88.9 0.8 turn.1
  89.7 1.6 %collective-permute-start.13 = (f32[128,640]{1,0:T(8,128)S(1)}, f32[128,640]{1,0:T(8,128)S(1)}, u32[]{:S(2)}, u32[]{:S(2)}) collective-permute-start(f32[128,640]{1,0:T(8,128)S(1)} %get-tuple-element.65), channel_id=1, source_target_pairs={{0,64},{64,0},{1,65},{65,1},{2,66},{66,2},{3,67},{67,3},{4,68},{68... | collective-permute-start | bytes 983048 | tf_op jit(solution)/shard_map/ppermute | solution.py:25
  91.3 0.6 collective-permute-start.12
  91.9 1.3 %collective-permute-start.14 = (bf16[128,640]{1,0:T(8,128)(2,1)S(1)}, bf16[128,640]{1,0:T(8,128)(2,1)S(1)}, u32[]{:S(2)}, u32[]{:S(2)}) collective-permute-start(bf16[128,640]{1,0:T(8,128)(2,1)S(1)} %get-tuple-element.66), channel_id=1, source_target_pairs={{0,65},{1,66},{2,67},{3,64},{4,69},{5,70},{6,71},{7,68},{64,1},{65... | collective-permute-start | bytes 491528 | tf_op jit(solution)/shard_map/ppermute | solution.py:21
  93.2 2.5 %collective-permute-start.15 = (bf16[128,640]{1,0:T(8,128)(2,1)S(1)}, bf16[128,640]{1,0:T(8,128)(2,1)S(1)}, u32[]{:S(2)}, u32[]{:S(2)}) collective-permute-start(bf16[128,640]{1,0:T(8,128)(2,1)S(1)} %get-tuple-element.67), channel_id=1, source_target_pairs={{0,66},{1,67},{2,64},{3,65},{4,70},{5,71},{6,68},{7,69},{64,2},{65... | collective-permute-start | bytes 491528 | tf_op jit(solution)/shard_map/ppermute | solution.py:21
  95.7 1.3 %collective-permute-start.16 = (bf16[128,640]{1,0:T(8,128)(2,1)S(1)}, bf16[128,640]{1,0:T(8,128)(2,1)S(1)}, u32[]{:S(2)}, u32[]{:S(2)}) collective-permute-start(bf16[128,640]{1,0:T(8,128)(2,1)S(1)} %get-tuple-element.68), channel_id=1, source_target_pairs={{0,67},{1,64},{2,65},{3,66},{4,71},{5,68},{6,69},{7,70},{64,3},{65... | collective-permute-start | bytes 491528 | tf_op jit(solution)/shard_map/ppermute | solution.py:21
  97.0 1.6 %collective-permute-done.12.x_ref = bf16[128,640]{1,0:T(8,128)(2,1)S(1)} collective-permute-done((bf16[128,640]{1,0:T(8,128)(2,1)S(1)}, bf16[128,640]{1,0:T(8,128)(2,1)S(1)}, u32[]{:S(2)}, u32[]{:S(2)}) %collective-permute-start.12) | collective-permute-done | bytes 163872 | tf_op jit(solution)/shard_map/ppermute | solution.py:21
  98.6 0.7 collective-permute-done.14.refs_0_
  99.2 4.4 %collective-permute-done.15.refs_1_ = bf16[128,640]{1,0:T(8,128)(2,1)S(1)} collective-permute-done((bf16[128,640]{1,0:T(8,128)(2,1)S(1)}, bf16[128,640]{1,0:T(8,128)(2,1)S(1)}, u32[]{:S(2)}, u32[]{:S(2)}) %collective-permute-start.15) | collective-permute-done | bytes 163872 | tf_op jit(solution)/shard_map/ppermute | solution.py:21
  103.6 1.5 %collect.1 = bf16[256,640]{1,0:T(8,128)(2,1)} custom-call(s32[5]{0:T(128)S(1)} %stack.19.info_ref, f32[8,128]{1,0:T(8,128)S(1)} %get-tuple-element.51.level_ref, f32[128,640]{1,0:T(8,128)S(1)} %get-tuple-element.63.own_ref, bf16[128,640]{1,0:T(8,128)(2,1)S(1)} %collective-permute-done.12.x_ref, f32[128,640]{1,0:T(8,128)S(1)} %collective-permute-done.13.other_ref, ...), custom_call_target="tpu_custom_call" | custom-call | tf_op jit(solution)/shard_map/collect/pallas_call | solution.py:489
  (4 shorter events, 0.0 us)
Async XLA Ops:
  5.9 8.2 %collective-permute-start.2 = (bf16[2,256,2560]{2,1,0:T(8,128)(2,1)S(1)}, bf16[2,256,2560]{2,1,0:T(8,128)(2,1)S(1)}, u32[]{:S(2)}, u32[]{:S(2)}) collective-permute-start(bf16[2,256,2560]{2,1,0:T(8,128)(2,1)S(1)} %get-tuple-element.41), channel_id=1, source_target_pairs={{0,64},{64,0},{1,65},{65,1},{2,66},{66,2},{3,67},{67,3},{4,68},{68... | collective-permute-start | bytes 7864328 | tf_op jit(solution)/shard_map/ppermute | solution.py:25
  10.1 10.3 %collective-permute-start.6 = (f32[3,128,384]{2,1,0:T(8,128)S(1)}, f32[3,128,384]{2,1,0:T(8,128)S(1)}, u32[]{:S(2)}, u32[]{:S(2)}) collective-permute-start(f32[3,128,384]{2,1,0:T(8,128)S(1)} %get-tuple-element.47), channel_id=1, source_target_pairs={{0,64},{64,0},{1,65},{65,1},{2,66},{66,2},{3,67},{67,3},{4,68},{68... | collective-permute-start | bytes 1769480 | tf_op jit(solution)/shard_map/ppermute | solution.py:25
  13.5 7.6 %collective-permute-start.4 = (f32[3,128,384]{2,1,0:T(8,128)S(1)}, f32[3,128,384]{2,1,0:T(8,128)S(1)}, u32[]{:S(2)}, u32[]{:S(2)}) collective-permute-start(f32[3,128,384]{2,1,0:T(8,128)S(1)} %get-tuple-element.43), channel_id=1, source_target_pairs={{0,64},{64,0},{1,65},{65,1},{2,66},{66,2},{3,67},{67,3},{4,68},{68... | collective-permute-start | bytes 1769480 | tf_op jit(solution)/shard_map/ppermute | solution.py:25
  16.5 3.9 %collective-permute-start.5 = (f32[3,128,384]{2,1,0:T(8,128)S(1)}, f32[3,128,384]{2,1,0:T(8,128)S(1)}, u32[]{:S(2)}, u32[]{:S(2)}) collective-permute-start(f32[3,128,384]{2,1,0:T(8,128)S(1)} %get-tuple-element.45), channel_id=1, source_target_pairs={{0,64},{64,0},{1,65},{65,1},{2,66},{66,2},{3,67},{67,3},{4,68},{68... | collective-permute-start | bytes 1769480 | tf_op jit(solution)/shard_map/ppermute | solution.py:25
  18.2 2.9 %collective-permute-start.3 = (f32[3,128,384]{2,1,0:T(8,128)S(1)}, f32[3,128,384]{2,1,0:T(8,128)S(1)}, u32[]{:S(2)}, u32[]{:S(2)}) collective-permute-start(f32[3,128,384]{2,1,0:T(8,128)S(1)} %project.7), channel_id=1, source_target_pairs={{0,64},{64,0},{1,65},{65,1},{2,66},{66,2},{3,67},{67,3},{4,68},{68... | collective-permute-start | bytes 1769480 | tf_op jit(solution)/shard_map/ppermute | solution.py:25
  22.8 25.8 %all-to-all-start = ((bf16[8,704,128]{2,1,0:T(8,128)(2,1)}), bf16[8,704,128]{2,1,0:T(8,128)(2,1)S(1)}, u32[]{:S(2)}, u32[]{:S(2)}) async-start(bf16[8,704,128]{2,1,0:T(8,128)(2,1)} %join.3), calls=%async_computation | async-start | bytes 2883584 | tf_op jit(solution)/shard_map/all_to_all | solution.py:29
  28.8 23.7 %collective-permute-start = (bf16[384,2560]{1,0:T(8,128)(2,1)}, bf16[384,2560]{1,0:T(8,128)(2,1)S(1)}, u32[]{:S(2)}, u32[]{:S(2)}) collective-permute-start(bf16[384,2560]{1,0:T(8,128)(2,1)} %refs_0_.1), channel_id=1, source_target_pairs={{0,64},{64,0},{1,65},{65,1},{2,66},{66,2},{3,67},{67,3},{4,68},{68... | collective-permute-start | bytes 5898248 | tf_op jit(solution)/shard_map/ppermute | solution.py:25
  29.1 23.4 %collective-permute-start.1 = (bf16[384,2560]{1,0:T(8,128)(2,1)}, bf16[384,2560]{1,0:T(8,128)(2,1)}, u32[]{:S(2)}, u32[]{:S(2)}) collective-permute-start(bf16[384,2560]{1,0:T(8,128)(2,1)} %refs_1_.1), channel_id=1, source_target_pairs={{0,64},{64,0},{1,65},{65,1},{2,66},{66,2},{3,67},{67,3},{4,68},{68... | collective-permute-start | bytes 5898248 | tf_op jit(solution)/shard_map/ppermute | solution.py:25
  48.6 4.0 %collective-permute-start.7 = (bf16[8,704,128]{2,1,0:T(8,128)(2,1)S(1)}, bf16[8,704,128]{2,1,0:T(8,128)(2,1)S(1)}, u32[]{:S(2)}, u32[]{:S(2)}) collective-permute-start(bf16[8,704,128]{2,1,0:T(8,128)(2,1)S(1)} %all-to-all-done.refs_2_.refs_3_), channel_id=1, source_target_pairs={{0,64},{64,0},{1,65},{65,1},{2,66},{66,2},{3,67},{67,3},{4,68},{68... | collective-permute-start | bytes 4325384 | tf_op jit(solution)/shard_map/ppermute | solution.py:25
  68.9 20.0 %collective-permute-start.8 = (bf16[4,128,640]{2,1,0:T(8,128)(2,1)S(1)}, bf16[4,128,640]{2,1,0:T(8,128)(2,1)S(1)}, u32[]{:S(2)}, u32[]{:S(2)}) collective-permute-start(bf16[4,128,640]{2,1,0:T(8,128)(2,1)S(1)} %get-tuple-element.59), channel_id=1, source_target_pairs={{0,4},{1,5},{2,6},{3,7},{4,0},{5,1},{6,2},{7,3},{64,68},{65,69},{6... | collective-permute-start | bytes 1966088 | tf_op jit(solution)/shard_map/ppermute | solution.py:21
  71.4 8.9 %collective-permute-start.10 = (bf16[2,128,640]{2,1,0:T(8,128)(2,1)S(1)}, bf16[2,128,640]{2,1,0:T(8,128)(2,1)S(1)}, u32[]{:S(2)}, u32[]{:S(2)}) collective-permute-start(bf16[2,128,640]{2,1,0:T(8,128)(2,1)S(1)} %get-tuple-element.61), channel_id=1, source_target_pairs={{0,2},{1,3},{2,0},{3,1},{4,6},{5,7},{6,4},{7,5},{64,66},{65,67},{6... | collective-permute-start | bytes 983048 | tf_op jit(solution)/shard_map/ppermute | solution.py:21
  74.3 14.5 %collective-permute-start.11 = (bf16[2,128,640]{2,1,0:T(8,128)(2,1)S(1)}, bf16[2,128,640]{2,1,0:T(8,128)(2,1)S(1)}, u32[]{:S(2)}, u32[]{:S(2)}) collective-permute-start(bf16[2,128,640]{2,1,0:T(8,128)(2,1)S(1)} %get-tuple-element.62), channel_id=1, source_target_pairs={{0,3},{1,0},{2,1},{3,2},{4,7},{5,4},{6,5},{7,6},{64,67},{65,64},{6... | collective-permute-start | bytes 983048 | tf_op jit(solution)/shard_map/ppermute | solution.py:21
  75.1 13.8 %collective-permute-start.9 = (bf16[2,128,640]{2,1,0:T(8,128)(2,1)S(1)}, bf16[2,128,640]{2,1,0:T(8,128)(2,1)S(1)}, u32[]{:S(2)}, u32[]{:S(2)}) collective-permute-start(bf16[2,128,640]{2,1,0:T(8,128)(2,1)S(1)} %get-tuple-element.60), channel_id=1, source_target_pairs={{0,1},{1,2},{2,3},{3,0},{4,5},{5,6},{6,7},{7,4},{64,65},{65,66},{6... | collective-permute-start | bytes 983048 | tf_op jit(solution)/shard_map/ppermute | solution.py:21
  89.7 13.9 %collective-permute-start.13 = (f32[128,640]{1,0:T(8,128)S(1)}, f32[128,640]{1,0:T(8,128)S(1)}, u32[]{:S(2)}, u32[]{:S(2)}) collective-permute-start(f32[128,640]{1,0:T(8,128)S(1)} %get-tuple-element.65), channel_id=1, source_target_pairs={{0,64},{64,0},{1,65},{65,1},{2,66},{66,2},{3,67},{67,3},{4,68},{68... | collective-permute-start | bytes 983048 | tf_op jit(solution)/shard_map/ppermute | solution.py:25
  91.3 7.3 %collective-permute-start.12 = (bf16[128,640]{1,0:T(8,128)(2,1)S(1)}, bf16[128,640]{1,0:T(8,128)(2,1)S(1)}, u32[]{:S(2)}, u32[]{:S(2)}) collective-permute-start(bf16[128,640]{1,0:T(8,128)(2,1)S(1)} %get-tuple-element.64), channel_id=1, source_target_pairs={{0,4},{1,5},{2,6},{3,7},{4,0},{5,1},{6,2},{7,3},{64,68},{65,69},{6... | collective-permute-start | bytes 491528 | tf_op jit(solution)/shard_map/ppermute | solution.py:21
  91.9 7.4 %collective-permute-start.14 = (bf16[128,640]{1,0:T(8,128)(2,1)S(1)}, bf16[128,640]{1,0:T(8,128)(2,1)S(1)}, u32[]{:S(2)}, u32[]{:S(2)}) collective-permute-start(bf16[128,640]{1,0:T(8,128)(2,1)S(1)} %get-tuple-element.66), channel_id=1, source_target_pairs={{0,65},{1,66},{2,67},{3,64},{4,69},{5,70},{6,71},{7,68},{64,1},{65... | collective-permute-start | bytes 491528 | tf_op jit(solution)/shard_map/ppermute | solution.py:21
  93.2 10.4 %collective-permute-start.15 = (bf16[128,640]{1,0:T(8,128)(2,1)S(1)}, bf16[128,640]{1,0:T(8,128)(2,1)S(1)}, u32[]{:S(2)}, u32[]{:S(2)}) collective-permute-start(bf16[128,640]{1,0:T(8,128)(2,1)S(1)} %get-tuple-element.67), channel_id=1, source_target_pairs={{0,66},{1,67},{2,64},{3,65},{4,70},{5,71},{6,68},{7,69},{64,2},{65... | collective-permute-start | bytes 491528 | tf_op jit(solution)/shard_map/ppermute | solution.py:21
  95.7 7.9 %collective-permute-start.16 = (bf16[128,640]{1,0:T(8,128)(2,1)S(1)}, bf16[128,640]{1,0:T(8,128)(2,1)S(1)}, u32[]{:S(2)}, u32[]{:S(2)}) collective-permute-start(bf16[128,640]{1,0:T(8,128)(2,1)S(1)} %get-tuple-element.68), channel_id=1, source_target_pairs={{0,67},{1,64},{2,65},{3,66},{4,71},{5,68},{6,69},{7,70},{64,3},{65... | collective-permute-start | bytes 491528 | tf_op jit(solution)/shard_map/ppermute | solution.py:21

commit v4 on v3

--- a/solution.py
+++ b/solution.py
@@ -142,7 +142,7 @@
 
 def norm(info, clean, noise, gt, gc, w):
     tokens, width = clean.shape
-    rows = 32
+    rows = 64
     count = tokens // rows
     tiles = (width // HD, HD)
     shape = ((2, tokens, width // 2), BF16)
@@ -236,13 +236,14 @@
         inputs, rest = refs[: len(parts)], refs[len(parts) :]
         copies = []
 
-        def leave(source, model, which):
+        def leave(source, model, which, base, size):
+            lines = pl.ds(base, size)
             clip = info_ref[AT_CORE] if which == 0 else 1 - info_ref[AT_CORE]
             copies.append(
                 pltpu.make_async_copy(
-                    source.at[pl.ds(2 * which, 2)],
-                    target.at[pl.ds(4 * model + 2 * clip, 2)],
-                    sem.at[2 * model + which],
+                    source.at[pl.ds(2 * which, 2), lines],
+                    target.at[pl.ds(4 * model + 2 * clip, 2), lines],
+                    sem.at[len(copies)],
                 )
             )
             copies[-1].start()
@@ -251,8 +252,8 @@
             (out,) = rest
         else:
             teacher, target, out, sem = rest
-            leave(teacher, 0, 0)
-            leave(teacher, 0, 1)
+            leave(teacher, 0, 0, 0, shape[1])
+            leave(teacher, 0, 1, 0, shape[1])
         for which in range(2):
             left, right = inputs[2 * which : 2 * which + 2]
             for kind, base in ((1, 0), (2, 2 * rows), (0, 4 * rows)):
@@ -264,8 +265,8 @@
                     if kind == 0:
                         middle = middle[j * half : (j + 1) * half]
                     out[block, base + rows : base + rows + middle.shape[0]] = middle
-            if done is not None:
-                leave(out, 1, which)
+                if done is not None:
+                    leave(out, 1, which, base, rows + middle.shape[0])
         for copy in copies:
             copy.wait()
 
@@ -281,7 +282,7 @@
         60 * rows * panel,
         scratch=()
         if done is None
-        else (pltpu.VMEM(part, BF16), pltpu.SemaphoreType.DMA((4,))),
+        else (pltpu.VMEM(part, BF16), pltpu.SemaphoreType.DMA((8,))),
         loose=() if done is None else ((shape, BF16),),
     )[0]
 
@@ -473,17 +474,20 @@
 
 def collect(info, level, own, from_x, other, from_y):
     rows, width = own.shape
+    step = 32
 
     def body(info_ref, level_ref, own_ref, x_ref, other_ref, *refs):
         y_refs, out_ref = refs[:-1], refs[-1]
         level = level_ref[:1, :1]
         core = info_ref[AT_CORE]
         for part, terms in ((core, (own_ref, x_ref)), (1 - core, (other_ref, *y_refs))):
-            total = terms[0][...]
-            for ref in terms[1:]:
-                total = total + ref[...].astype(F32)
-            place = pl.ds(pl.multiple_of(part * rows, rows), rows)
-            out_ref[place, :] = (level * total).astype(BF16)
+            for line in range(0, rows, step):
+                lines = slice(line, line + step)
+                total = terms[0][lines, :]
+                for ref in terms[1:]:
+                    total = total + ref[lines, :].astype(F32)
+                place = pl.ds(pl.multiple_of(part * rows + line, step), step)
+                out_ref[place, :] = (level * total).astype(BF16)
 
     operands = (level, own, from_x, other, *from_y)
     return pl.pallas_call(

time: 105 us -> 105 us (level)
  no operation moved by 1% of the time
where the time goes in v4:
time: 105 us
  waiting for transfers between devices  37.3 us (36%)
  Pallas kernels  31.3 us (30%)
  starting transfers between devices  24.7 us (24%)
  blocking collectives  10.7 us (10%)
    pallas_call x13, Pallas kernels, kernel(): pl.pallas_call(body, in_specs=[SCALAR] + [ANYWHERE] * len(far) + [NEAR] *...  29.9 us
    all_to_all x1, waiting for transfers between devices, exchange(): return lax.all_to_all(value, axes, 0, 0, tiled=True)  19.3 us
    ppermute x8, waiting for transfers between devices, over_tp(): return lax.ppermute(value, ('dp', 'tp'), pairs)  18 us
    ppermute x8, starting transfers between devices, over_tp(): return lax.ppermute(value, ('dp', 'tp'), pairs)  12.6 us
    all_to_all x1, blocking collectives, exchange(): return lax.all_to_all(value, axes, 0, 0, tiled=True)  10.7 us
    ppermute x9, starting transfers between devices, swapped(): return lax.ppermute(value, 'dp', [(0, 1), (1, 0)])  6.08 us
    all_to_all x1, starting transfers between devices, exchange(): return lax.all_to_all(value, axes, 0, 0, tiled=True)  6.05 us
  transfers between devices with their start and end apart: 18, of which 6 were waited for; matrix products, arithmetic and copies ran while one was open for 0% of the time, Pallas kernels for 16%

profile of v4, /device:TPU:1, one launch (start us, length us, event | category | flops | bytes accessed | tf_op | source)
XLA Modules:
  0.0 104.9 jit_solution(7648804207522944820)
XLA Ops:
  0.7 0.1 stack.19.info_ref
  0.7 4.9 %norm.1 = (bf16[2,256,2560]{2,1,0:T(8,128)(2,1)S(1)}, bf16[2,256,2560]{2,1,0:T(8,128)(2,1)S(1)}, bf16[3,2560,384]{2,1,0:T(8,128)(2,1)S(1)}) custom-call(s32[5]{0:T(128)S(1)} %stack.19.info_ref, bf16[256,5120]{1,0:T(8,128)(2,1)} %bitcast.14, bf16[256,5120]{1,0:T(8,128)(2,1)} %bitcast.15, f32[40,128]{1,0:T(8,128)} %bitcast.16, f32[40,128]{1,0:T(8,128)} %bitcast.17, ...), custom_call_target="tpu_custom_call" | custom-call | flops 13107200 | bytes 10485760 | tf_op jit(solution)/shard_map/norm/pallas_call | solution.py:46
  5.7 1.5 %collective-permute-start.2 = (bf16[2,256,2560]{2,1,0:T(8,128)(2,1)S(1)}, bf16[2,256,2560]{2,1,0:T(8,128)(2,1)S(1)}, u32[]{:S(2)}, u32[]{:S(2)}) collective-permute-start(bf16[2,256,2560]{2,1,0:T(8,128)(2,1)S(1)} %get-tuple-element.41), channel_id=1, source_target_pairs={{0,64},{64,0},{1,65},{65,1},{2,66},{66,2},{3,67},{67,3},{4,68},{68... | collective-permute-start | bytes 7864328 | tf_op jit(solution)/shard_map/ppermute | solution.py:25
  7.2 2.7 %project.5 = (f32[3,128,384]{2,1,0:T(8,128)S(1)}, f32[3,128,384]{2,1,0:T(8,128)S(1)}, bf16[2,2560,384]{2,1,0:T(8,128)(2,1)S(1)}) custom-call(s32[5]{0:T(128)S(1)} %stack.19.info_ref, bf16[3,2560,384]{2,1,0:T(8,128)(2,1)} %bitcast.11, bf16[2,256,2560]{2,1,0:T(8,128)(2,1)S(1)} %get-tuple-element.37.refs_1_, ...), custom_call_target="tpu_custom_call" | custom-call | flops 1509949440 | bytes 7208960 | tf_op jit(solution)/shard_map/project/pallas_call | solution.py:46
  9.9 0.1 collective-permute-start.6
  10.0 3.3 %project.6 = (f32[3,128,384]{2,1,0:T(8,128)S(1)}, f32[3,128,384]{2,1,0:T(8,128)S(1)}, bf16[1,2560,384]{2,1,0:T(8,128)(2,1)S(1)}) custom-call(s32[5]{0:T(128)S(1)} %stack.19.info_ref, bf16[3,2560,384]{2,1,0:T(8,128)(2,1)} %bitcast.12, bf16[2,256,2560]{2,1,0:T(8,128)(2,1)S(1)} %get-tuple-element.37.refs_1_, ...), custom_call_target="tpu_custom_call" | custom-call | flops 1509949440 | bytes 7208960 | tf_op jit(solution)/shard_map/project/pallas_call | solution.py:46
  13.3 0.6 collective-permute-start.4
  13.9 0.0 collective-permute-done.2.refs_0_
  13.9 2.4 %project.9 = (f32[3,128,384]{2,1,0:T(8,128)S(1)}, f32[3,128,384]{2,1,0:T(8,128)S(1)}) custom-call(s32[5]{0:T(128)S(1)} %stack.19.info_ref, bf16[2,256,2560]{2,1,0:T(8,128)(2,1)S(1)} %collective-permute-done.2.refs_0_, bf16[3,2560,384]{2,1,0:T(8,128)(2,1)S(1)} %get-tuple-element.38.refs_2_.refs_1_), custom_call_target="tpu_custom_call" | custom-call | flops 1509949440 | bytes 7208960 | tf_op jit(solution)/shard_map/project/pallas_call | solution.py:46
  16.3 0.1 collective-permute-start.5
  16.4 1.6 %project.7 = f32[3,128,384]{2,1,0:T(8,128)S(1)} custom-call(s32[5]{0:T(128)S(1)} %stack.19.info_ref, bf16[2,256,2560]{2,1,0:T(8,128)(2,1)S(1)} %collective-permute-done.2.refs_0_, bf16[2,2560,384]{2,1,0:T(8,128)(2,1)S(1)} %get-tuple-element.39.refs_2_.refs_1_, bf16[1,2560,384]{2,1,0:T(8,128)(2,1)S(1)} %get-tuple-element.42.refs_2_), custom_call_target="tpu_custom_call" | custom-call | flops 754974720 | bytes 7208960 | tf_op jit(solution)/shard_map/project/pallas_call | solution.py:46
  18.0 0.6 collective-permute-start.3
  18.6 1.6 %project.8.refs_2_ = f32[3,128,384]{2,1,0:T(8,128)S(1)} custom-call(s32[5]{0:T(128)S(1)} %stack.19.info_ref, bf16[2,256,2560]{2,1,0:T(8,128)(2,1)S(1)} %collective-permute-done.2.refs_0_, bf16[2,2560,384]{2,1,0:T(8,128)(2,1)S(1)} %get-tuple-element.39.refs_2_.refs_1_, bf16[1,2560,384]{2,1,0:T(8,128)(2,1)S(1)} %get-tuple-element.42.refs_2_), custom_call_target="tpu_custom_call" | custom-call | flops 754974720 | bytes 7208960 | tf_op jit(solution)/shard_map/project/pallas_call | solution.py:46
  20.2 0.0 collective-permute-done.6.refs_3_
  20.2 0.7 join.2.refs_4_
  20.9 0.0 collective-permute-done.4.refs_3_
  20.9 1.8 %join.3 = bf16[8,704,128]{2,1,0:T(8,128)(2,1)} custom-call(s32[5]{0:T(128)S(1)} %stack.19.info_ref, f32[3,128,384]{2,1,0:T(8,128)S(1)} %get-tuple-element.40.refs_0_, f32[3,128,384]{2,1,0:T(8,128)S(1)} %collective-permute-done.3.refs_1_, f32[3,128,384]{2,1,0:T(8,128)S(1)} %project.8.refs_2_, f32[3,128,384]{2,1,0:T(8,128)S(1)} %collective-permute-done.4.refs_3_, ...), custom_call_target="tpu_custom_call" | custom-call | flops 294912 | bytes 2949120 | tf_op jit(solution)/shard_map/join/pallas_call | solution.py:46
  22.7 6.1 %all-to-all-start = ((bf16[8,704,128]{2,1,0:T(8,128)(2,1)}), bf16[8,704,128]{2,1,0:T(8,128)(2,1)S(1)}, u32[]{:S(2)}, u32[]{:S(2)}) async-start(bf16[8,704,128]{2,1,0:T(8,128)(2,1)} %join.3), calls=%async_computation | async-start | bytes 2883584 | tf_op jit(solution)/shard_map/all_to_all | solution.py:29
  28.7 0.3 collective-permute-start
  29.0 0.2 collective-permute-start.1
  29.2 19.3 %all-to-all-done.refs_2_.refs_3_ = bf16[8,704,128]{2,1,0:T(8,128)(2,1)S(1)} async-done(((bf16[8,704,128]{2,1,0:T(8,128)(2,1)}), bf16[8,704,128]{2,1,0:T(8,128)(2,1)S(1)}, u32[]{:S(2)}, u32[]{:S(2)}) %all-to-all-start) | async-done | bytes 1441824 | tf_op jit(solution)/shard_map/all_to_all | solution.py:29
  48.5 1.1 %collective-permute-start.7 = (bf16[8,704,128]{2,1,0:T(8,128)(2,1)S(1)}, bf16[8,704,128]{2,1,0:T(8,128)(2,1)S(1)}, u32[]{:S(2)}, u32[]{:S(2)}) collective-permute-start(bf16[8,704,128]{2,1,0:T(8,128)(2,1)S(1)} %all-to-all-done.refs_2_.refs_3_), channel_id=1, source_target_pairs={{0,64},{64,0},{1,65},{65,1},{2,66},{66,2},{3,67},{67,3},{4,68},{68... | collective-permute-start | bytes 4325384 | tf_op jit(solution)/shard_map/ppermute | solution.py:25
  49.6 2.8 %attend.2 = (bf16[384,2560]{1,0:T(8,128)(2,1)S(1)}, bf16[384,2560]{1,0:T(8,128)(2,1)S(1)}, f32[1536,128]{1,0:T(8,128)S(1)}, f32[1536,128]{1,0:T(8,128)S(1)}, f32[1536,128]{1,0:T(8,128)S(1)}) custom-call(s32[5]{0:T(128)S(1)} %stack.19.info_ref, bf16[384,2560]{1,0:T(8,128)(2,1)} %refs_0_.1, bf16[384,2560]{1,0:T(8,128)(2,1)} %refs_1_.1, ...), custom_call_target="tpu_custom_call" | custom-call | flops 805306368 | bytes 1310720 | tf_op jit(solution)/shard_map/attend/pallas_call | solution.py:46
  52.4 0.0 collective-permute-done.refs_0_
  52.5 0.0 collective-permute-done.7.refs_3_
  52.5 3.3 %attend.3 = (bf16[384,2560]{1,0:T(8,128)(2,1)S(1)}, bf16[384,2560]{1,0:T(8,128)(2,1)S(1)}, bf16[8,192,128]{2,1,0:T(8,128)(2,1)S(1)}, f32[8,128]{1,0:T(8,128)S(1)}) custom-call(s32[5]{0:T(128)S(1)} %stack.19.info_ref, bf16[384,2560]{1,0:T(8,128)(2,1)S(1)} %collective-permute-done.refs_0_, bf16[384,2560]{1,0:T(8,128)(2,1)} %collective-permute-done.1.refs_1_, ...), custom_call_target="tpu_custom_call" | custom-call | flops 805306368 | bytes 1310720 | tf_op jit(solution)/shard_map/attend/pallas_call | solution.py:46
  55.8 10.7 %all_to_all.10.attn_ref = bf16[8,192,128]{2,1,0:T(8,128)(2,1)S(1)} all-to-all(bf16[8,192,128]{2,1,0:T(8,128)(2,1)S(1)} %get-tuple-element.52), channel_id=1, replica_groups=mesh['dp'=2,'ctx'=8,'tp'=8] {'ctx'}, dimensions={0} | all-to-all | bytes 786432 | tf_op jit(solution)/shard_map/all_to_all | solution.py:29
  66.5 2.3 %expand.3 = (bf16[4,128,640]{2,1,0:T(8,128)(2,1)S(1)}, bf16[2,128,640]{2,1,0:T(8,128)(2,1)S(1)}, bf16[2,128,640]{2,1,0:T(8,128)(2,1)S(1)}, bf16[2,128,640]{2,1,0:T(8,128)(2,1)S(1)}) custom-call(s32[5]{0:T(128)S(1)} %stack.19.info_ref, bf16[8,192,128]{2,1,0:T(8,128)(2,1)S(1)} %all_to_all.10.attn_ref, bf16[384,2560]{1,0:T(8,128)(2,1)S(1)} %get-tuple-element.53.refs_0_, ...), custom_call_target="tpu_custom_call" | custom-call | flops 1006632960 | bytes 7864320 | tf_op jit(solution)/shard_map/expand/pallas_call | solution.py:46
  68.8 2.5 %collective-permute-start.8 = (bf16[4,128,640]{2,1,0:T(8,128)(2,1)S(1)}, bf16[4,128,640]{2,1,0:T(8,128)(2,1)S(1)}, u32[]{:S(2)}, u32[]{:S(2)}) collective-permute-start(bf16[4,128,640]{2,1,0:T(8,128)(2,1)S(1)} %get-tuple-element.59), channel_id=1, source_target_pairs={{0,4},{1,5},{2,6},{3,7},{4,0},{5,1},{6,2},{7,3},{64,68},{65,69},{6... | collective-permute-start | bytes 1966088 | tf_op jit(solution)/shard_map/ppermute | solution.py:21
  71.3 2.9 %collective-permute-start.10 = (bf16[2,128,640]{2,1,0:T(8,128)(2,1)S(1)}, bf16[2,128,640]{2,1,0:T(8,128)(2,1)S(1)}, u32[]{:S(2)}, u32[]{:S(2)}) collective-permute-start(bf16[2,128,640]{2,1,0:T(8,128)(2,1)S(1)} %get-tuple-element.61), channel_id=1, source_target_pairs={{0,2},{1,3},{2,0},{3,1},{4,6},{5,7},{6,4},{7,5},{64,66},{65,67},{6... | collective-permute-start | bytes 983048 | tf_op jit(solution)/shard_map/ppermute | solution.py:21
  74.2 0.8 collective-permute-start.11
  75.0 0.7 collective-permute-start.9
  75.7 1.7 %expand.2 = (f32[4,128,640]{2,1,0:T(8,128)S(1)}, f32[2,128,640]{2,1,0:T(8,128)S(1)}) custom-call(s32[5]{0:T(128)S(1)} %stack.19.info_ref, bf16[8,192,128]{2,1,0:T(8,128)(2,1)S(1)} %all_to_all.10.attn_ref, bf16[384,2560]{1,0:T(8,128)(2,1)S(1)} %get-tuple-element.53.refs_0_, bf16[384,2560]{1,0:T(8,128)(2,1)S(1)} %get-tuple-element.54.refs_1_, ...), custom_call_target="tpu_custom_call" | custom-call | flops 1006632960 | bytes 7864320 | tf_op jit(solution)/shard_map/expand/pallas_call | solution.py:46
  77.4 2.8 %collective-permute-done.10.refs_1_ = bf16[2,128,640]{2,1,0:T(8,128)(2,1)S(1)} collective-permute-done((bf16[2,128,640]{2,1,0:T(8,128)(2,1)S(1)}, bf16[2,128,640]{2,1,0:T(8,128)(2,1)S(1)}, u32[]{:S(2)}, u32[]{:S(2)}) %collective-permute-start.10) | collective-permute-done | bytes 327712 | tf_op jit(solution)/shard_map/ppermute | solution.py:21
  80.2 8.5 %collective-permute-done.11.refs_2_ = bf16[2,128,640]{2,1,0:T(8,128)(2,1)S(1)} collective-permute-done((bf16[2,128,640]{2,1,0:T(8,128)(2,1)S(1)}, bf16[2,128,640]{2,1,0:T(8,128)(2,1)S(1)}, u32[]{:S(2)}, u32[]{:S(2)}) %collective-permute-start.11) | collective-permute-done | bytes 327712 | tf_op jit(solution)/shard_map/ppermute | solution.py:21
  88.7 0.0 collective-permute-done.9.refs_0_
  88.8 0.8 turn.1
  89.6 1.6 %collective-permute-start.13 = (f32[128,640]{1,0:T(8,128)S(1)}, f32[128,640]{1,0:T(8,128)S(1)}, u32[]{:S(2)}, u32[]{:S(2)}) collective-permute-start(f32[128,640]{1,0:T(8,128)S(1)} %get-tuple-element.65), channel_id=1, source_target_pairs={{0,64},{64,0},{1,65},{65,1},{2,66},{66,2},{3,67},{67,3},{4,68},{68... | collective-permute-start | bytes 983048 | tf_op jit(solution)/shard_map/ppermute | solution.py:25
  91.2 0.5 collective-permute-start.12
  91.7 1.3 %collective-permute-start.14 = (bf16[128,640]{1,0:T(8,128)(2,1)S(1)}, bf16[128,640]{1,0:T(8,128)(2,1)S(1)}, u32[]{:S(2)}, u32[]{:S(2)}) collective-permute-start(bf16[128,640]{1,0:T(8,128)(2,1)S(1)} %get-tuple-element.66), channel_id=1, source_target_pairs={{0,65},{1,66},{2,67},{3,64},{4,69},{5,70},{6,71},{7,68},{64,1},{65... | collective-permute-start | bytes 491528 | tf_op jit(solution)/shard_map/ppermute | solution.py:21
  93.0 2.5 %collective-permute-start.15 = (bf16[128,640]{1,0:T(8,128)(2,1)S(1)}, bf16[128,640]{1,0:T(8,128)(2,1)S(1)}, u32[]{:S(2)}, u32[]{:S(2)}) collective-permute-start(bf16[128,640]{1,0:T(8,128)(2,1)S(1)} %get-tuple-element.67), channel_id=1, source_target_pairs={{0,66},{1,67},{2,64},{3,65},{4,70},{5,71},{6,68},{7,69},{64,2},{65... | collective-permute-start | bytes 491528 | tf_op jit(solution)/shard_map/ppermute | solution.py:21
  95.5 1.3 %collective-permute-start.16 = (bf16[128,640]{1,0:T(8,128)(2,1)S(1)}, bf16[128,640]{1,0:T(8,128)(2,1)S(1)}, u32[]{:S(2)}, u32[]{:S(2)}) collective-permute-start(bf16[128,640]{1,0:T(8,128)(2,1)S(1)} %get-tuple-element.68), channel_id=1, source_target_pairs={{0,67},{1,64},{2,65},{3,66},{4,71},{5,68},{6,69},{7,70},{64,3},{65... | collective-permute-start | bytes 491528 | tf_op jit(solution)/shard_map/ppermute | solution.py:21
  96.9 1.6 %collective-permute-done.12.x_ref = bf16[128,640]{1,0:T(8,128)(2,1)S(1)} collective-permute-done((bf16[128,640]{1,0:T(8,128)(2,1)S(1)}, bf16[128,640]{1,0:T(8,128)(2,1)S(1)}, u32[]{:S(2)}, u32[]{:S(2)}) %collective-permute-start.12) | collective-permute-done | bytes 163872 | tf_op jit(solution)/shard_map/ppermute | solution.py:21
  98.4 0.7 collective-permute-done.14.refs_0_
  99.1 4.4 %collective-permute-done.15.refs_1_ = bf16[128,640]{1,0:T(8,128)(2,1)S(1)} collective-permute-done((bf16[128,640]{1,0:T(8,128)(2,1)S(1)}, bf16[128,640]{1,0:T(8,128)(2,1)S(1)}, u32[]{:S(2)}, u32[]{:S(2)}) %collective-permute-start.15) | collective-permute-done | bytes 163872 | tf_op jit(solution)/shard_map/ppermute | solution.py:21
  103.5 0.0 collective-permute-done.16.refs_2_
  103.5 0.0 collective-permute-done.13.other_ref
  103.5 1.4 %collect.1 = bf16[256,640]{1,0:T(8,128)(2,1)} custom-call(s32[5]{0:T(128)S(1)} %stack.19.info_ref, f32[8,128]{1,0:T(8,128)S(1)} %get-tuple-element.51.level_ref, f32[128,640]{1,0:T(8,128)S(1)} %get-tuple-element.63.own_ref, bf16[128,640]{1,0:T(8,128)(2,1)S(1)} %collective-permute-done.12.x_ref, f32[128,640]{1,0:T(8,128)S(1)} %collective-permute-done.13.other_ref, ...), custom_call_target="tpu_custom_call" | custom-call | tf_op jit(solution)/shard_map/collect/pallas_call | solution.py:493
  (4 shorter events, 0.0 us)
Async XLA Ops:
  5.7 8.2 %collective-permute-start.2 = (bf16[2,256,2560]{2,1,0:T(8,128)(2,1)S(1)}, bf16[2,256,2560]{2,1,0:T(8,128)(2,1)S(1)}, u32[]{:S(2)}, u32[]{:S(2)}) collective-permute-start(bf16[2,256,2560]{2,1,0:T(8,128)(2,1)S(1)} %get-tuple-element.41), channel_id=1, source_target_pairs={{0,64},{64,0},{1,65},{65,1},{2,66},{66,2},{3,67},{67,3},{4,68},{68... | collective-permute-start | bytes 7864328 | tf_op jit(solution)/shard_map/ppermute | solution.py:25
  9.9 10.3 %collective-permute-start.6 = (f32[3,128,384]{2,1,0:T(8,128)S(1)}, f32[3,128,384]{2,1,0:T(8,128)S(1)}, u32[]{:S(2)}, u32[]{:S(2)}) collective-permute-start(f32[3,128,384]{2,1,0:T(8,128)S(1)} %get-tuple-element.47), channel_id=1, source_target_pairs={{0,64},{64,0},{1,65},{65,1},{2,66},{66,2},{3,67},{67,3},{4,68},{68... | collective-permute-start | bytes 1769480 | tf_op jit(solution)/shard_map/ppermute | solution.py:25
  13.3 7.6 %collective-permute-start.4 = (f32[3,128,384]{2,1,0:T(8,128)S(1)}, f32[3,128,384]{2,1,0:T(8,128)S(1)}, u32[]{:S(2)}, u32[]{:S(2)}) collective-permute-start(f32[3,128,384]{2,1,0:T(8,128)S(1)} %get-tuple-element.43), channel_id=1, source_target_pairs={{0,64},{64,0},{1,65},{65,1},{2,66},{66,2},{3,67},{67,3},{4,68},{68... | collective-permute-start | bytes 1769480 | tf_op jit(solution)/shard_map/ppermute | solution.py:25
  16.3 3.9 %collective-permute-start.5 = (f32[3,128,384]{2,1,0:T(8,128)S(1)}, f32[3,128,384]{2,1,0:T(8,128)S(1)}, u32[]{:S(2)}, u32[]{:S(2)}) collective-permute-start(f32[3,128,384]{2,1,0:T(8,128)S(1)} %get-tuple-element.45), channel_id=1, source_target_pairs={{0,64},{64,0},{1,65},{65,1},{2,66},{66,2},{3,67},{67,3},{4,68},{68... | collective-permute-start | bytes 1769480 | tf_op jit(solution)/shard_map/ppermute | solution.py:25
  18.0 2.9 %collective-permute-start.3 = (f32[3,128,384]{2,1,0:T(8,128)S(1)}, f32[3,128,384]{2,1,0:T(8,128)S(1)}, u32[]{:S(2)}, u32[]{:S(2)}) collective-permute-start(f32[3,128,384]{2,1,0:T(8,128)S(1)} %project.7), channel_id=1, source_target_pairs={{0,64},{64,0},{1,65},{65,1},{2,66},{66,2},{3,67},{67,3},{4,68},{68... | collective-permute-start | bytes 1769480 | tf_op jit(solution)/shard_map/ppermute | solution.py:25
  22.7 25.9 %all-to-all-start = ((bf16[8,704,128]{2,1,0:T(8,128)(2,1)}), bf16[8,704,128]{2,1,0:T(8,128)(2,1)S(1)}, u32[]{:S(2)}, u32[]{:S(2)}) async-start(bf16[8,704,128]{2,1,0:T(8,128)(2,1)} %join.3), calls=%async_computation | async-start | bytes 2883584 | tf_op jit(solution)/shard_map/all_to_all | solution.py:29
  28.7 23.7 %collective-permute-start = (bf16[384,2560]{1,0:T(8,128)(2,1)}, bf16[384,2560]{1,0:T(8,128)(2,1)S(1)}, u32[]{:S(2)}, u32[]{:S(2)}) collective-permute-start(bf16[384,2560]{1,0:T(8,128)(2,1)} %refs_0_.1), channel_id=1, source_target_pairs={{0,64},{64,0},{1,65},{65,1},{2,66},{66,2},{3,67},{67,3},{4,68},{68... | collective-permute-start | bytes 5898248 | tf_op jit(solution)/shard_map/ppermute | solution.py:25
  29.0 23.4 %collective-permute-start.1 = (bf16[384,2560]{1,0:T(8,128)(2,1)}, bf16[384,2560]{1,0:T(8,128)(2,1)}, u32[]{:S(2)}, u32[]{:S(2)}) collective-permute-start(bf16[384,2560]{1,0:T(8,128)(2,1)} %refs_1_.1), channel_id=1, source_target_pairs={{0,64},{64,0},{1,65},{65,1},{2,66},{66,2},{3,67},{67,3},{4,68},{68... | collective-permute-start | bytes 5898248 | tf_op jit(solution)/shard_map/ppermute | solution.py:25
  48.5 4.0 %collective-permute-start.7 = (bf16[8,704,128]{2,1,0:T(8,128)(2,1)S(1)}, bf16[8,704,128]{2,1,0:T(8,128)(2,1)S(1)}, u32[]{:S(2)}, u32[]{:S(2)}) collective-permute-start(bf16[8,704,128]{2,1,0:T(8,128)(2,1)S(1)} %all-to-all-done.refs_2_.refs_3_), channel_id=1, source_target_pairs={{0,64},{64,0},{1,65},{65,1},{2,66},{66,2},{3,67},{67,3},{4,68},{68... | collective-permute-start | bytes 4325384 | tf_op jit(solution)/shard_map/ppermute | solution.py:25
  68.8 20.0 %collective-permute-start.8 = (bf16[4,128,640]{2,1,0:T(8,128)(2,1)S(1)}, bf16[4,128,640]{2,1,0:T(8,128)(2,1)S(1)}, u32[]{:S(2)}, u32[]{:S(2)}) collective-permute-start(bf16[4,128,640]{2,1,0:T(8,128)(2,1)S(1)} %get-tuple-element.59), channel_id=1, source_target_pairs={{0,4},{1,5},{2,6},{3,7},{4,0},{5,1},{6,2},{7,3},{64,68},{65,69},{6... | collective-permute-start | bytes 1966088 | tf_op jit(solution)/shard_map/ppermute | solution.py:21
  71.3 9.0 %collective-permute-start.10 = (bf16[2,128,640]{2,1,0:T(8,128)(2,1)S(1)}, bf16[2,128,640]{2,1,0:T(8,128)(2,1)S(1)}, u32[]{:S(2)}, u32[]{:S(2)}) collective-permute-start(bf16[2,128,640]{2,1,0:T(8,128)(2,1)S(1)} %get-tuple-element.61), channel_id=1, source_target_pairs={{0,2},{1,3},{2,0},{3,1},{4,6},{5,7},{6,4},{7,5},{64,66},{65,67},{6... | collective-permute-start | bytes 983048 | tf_op jit(solution)/shard_map/ppermute | solution.py:21
  74.2 14.5 %collective-permute-start.11 = (bf16[2,128,640]{2,1,0:T(8,128)(2,1)S(1)}, bf16[2,128,640]{2,1,0:T(8,128)(2,1)S(1)}, u32[]{:S(2)}, u32[]{:S(2)}) collective-permute-start(bf16[2,128,640]{2,1,0:T(8,128)(2,1)S(1)} %get-tuple-element.62), channel_id=1, source_target_pairs={{0,3},{1,0},{2,1},{3,2},{4,7},{5,4},{6,5},{7,6},{64,67},{65,64},{6... | collective-permute-start | bytes 983048 | tf_op jit(solution)/shard_map/ppermute | solution.py:21
  75.0 13.8 %collective-permute-start.9 = (bf16[2,128,640]{2,1,0:T(8,128)(2,1)S(1)}, bf16[2,128,640]{2,1,0:T(8,128)(2,1)S(1)}, u32[]{:S(2)}, u32[]{:S(2)}) collective-permute-start(bf16[2,128,640]{2,1,0:T(8,128)(2,1)S(1)} %get-tuple-element.60), channel_id=1, source_target_pairs={{0,1},{1,2},{2,3},{3,0},{4,5},{5,6},{6,7},{7,4},{64,65},{65,66},{6... | collective-permute-start | bytes 983048 | tf_op jit(solution)/shard_map/ppermute | solution.py:21
  89.6 13.9 %collective-permute-start.13 = (f32[128,640]{1,0:T(8,128)S(1)}, f32[128,640]{1,0:T(8,128)S(1)}, u32[]{:S(2)}, u32[]{:S(2)}) collective-permute-start(f32[128,640]{1,0:T(8,128)S(1)} %get-tuple-element.65), channel_id=1, source_target_pairs={{0,64},{64,0},{1,65},{65,1},{2,66},{66,2},{3,67},{67,3},{4,68},{68... | collective-permute-start | bytes 983048 | tf_op jit(solution)/shard_map/ppermute | solution.py:25
  91.2 7.3 %collective-permute-start.12 = (bf16[128,640]{1,0:T(8,128)(2,1)S(1)}, bf16[128,640]{1,0:T(8,128)(2,1)S(1)}, u32[]{:S(2)}, u32[]{:S(2)}) collective-permute-start(bf16[128,640]{1,0:T(8,128)(2,1)S(1)} %get-tuple-element.64), channel_id=1, source_target_pairs={{0,4},{1,5},{2,6},{3,7},{4,0},{5,1},{6,2},{7,3},{64,68},{65,69},{6... | collective-permute-start | bytes 491528 | tf_op jit(solution)/shard_map/ppermute | solution.py:21
  91.7 7.4 %collective-permute-start.14 = (bf16[128,640]{1,0:T(8,128)(2,1)S(1)}, bf16[128,640]{1,0:T(8,128)(2,1)S(1)}, u32[]{:S(2)}, u32[]{:S(2)}) collective-permute-start(bf16[128,640]{1,0:T(8,128)(2,1)S(1)} %get-tuple-element.66), channel_id=1, source_target_pairs={{0,65},{1,66},{2,67},{3,64},{4,69},{5,70},{6,71},{7,68},{64,1},{65... | collective-permute-start | bytes 491528 | tf_op jit(solution)/shard_map/ppermute | solution.py:21
  93.0 10.4 %collective-permute-start.15 = (bf16[128,640]{1,0:T(8,128)(2,1)S(1)}, bf16[128,640]{1,0:T(8,128)(2,1)S(1)}, u32[]{:S(2)}, u32[]{:S(2)}) collective-permute-start(bf16[128,640]{1,0:T(8,128)(2,1)S(1)} %get-tuple-element.67), channel_id=1, source_target_pairs={{0,66},{1,67},{2,64},{3,65},{4,70},{5,71},{6,68},{7,69},{64,2},{65... | collective-permute-start | bytes 491528 | tf_op jit(solution)/shard_map/ppermute | solution.py:21
  95.5 7.9 %collective-permute-start.16 = (bf16[128,640]{1,0:T(8,128)(2,1)S(1)}, bf16[128,640]{1,0:T(8,128)(2,1)S(1)}, u32[]{:S(2)}, u32[]{:S(2)}) collective-permute-start(bf16[128,640]{1,0:T(8,128)(2,1)S(1)} %get-tuple-element.68), channel_id=1, source_target_pairs={{0,67},{1,64},{2,65},{3,66},{4,71},{5,68},{6,69},{7,70},{64,3},{65... | collective-permute-start | bytes 491528 | tf_op jit(solution)/shard_map/ppermute | solution.py:21
